TPU v7x, 768 devices: a whole 4x8x12 slice. The times are simulated.
768 devices in a mesh: row: 64 (over y, x, core), col: 12 (over z).
Axes of the slice: x: 4, y: 8, z: 12, core: 2. Of those that a mesh axis runs over, the one named last changes fastest.
Arguments:
- a_blocks: bfloat16 [1024, 1536, 128], P('row', 'col'), may hold values from -6 to 6
- b_blocks: bfloat16 [1024, 1536, 128], P('row', 'col'), may hold values from -0.125 to 0.125
- pair_a: int32 [3072, 192], P('row', 'col'), may hold values from 0 to 15
- pair_b: int32 [3072, 192], P('row', 'col'), may hold values from 0 to 16, as said below
- owner: int32 [18432, 1], P(('row', 'col')), may hold values from 0 to 11; in each aligned block of 24 rows (0 to 23, 24 to 47, ...) at most 4 rows name the same one
Outputs:
- owned: bfloat16 [36864, 128, 128], P(('row', 'col'))
Inputs may be any that keep to these rules, and one draw needn't show every extreme that they name: `pair_b`: entries equal to 16 are padding. In each product block and step the live pairs come first, at least one, and are distinct; some block of every device and step has all 16 live and some has padding. Among the 24 blocks of one device no owner is named more than 4 times.
All inputs are finite; a program needn't handle non-finite values.
Results may differ from a plain program's by a relative error of at most 0.0012.
Values may be sent and summed in bfloat16 or wider, within the bound.
No kernel may reach another device: no remote copies, remote signals or barrier semaphores. Data moves between devices by JAX's collectives and lax.ppermute only.
A program may use at most 64 MiB of HBM per device.

v0:
```python
import jax
import jax.numpy as jnp
from jax import lax
from jax.sharding import PartitionSpec as P

BS = 128
KP = 16
STEPS = 2


def broadcast(value, axis, source):
    kept = jnp.where(lax.axis_index(axis) == source, value, 0).astype(value.dtype)
    return lax.psum(kept, axis)


def step_products(a_panel, b_panel, picks_a, picks_b, summed, group):
    right_ext = jnp.concatenate([b_panel, jnp.zeros((1,) + b_panel.shape[1:], b_panel.dtype)], 0)

    def add_group(group_index, total):
        left_picks = lax.dynamic_slice_in_dim(picks_a, group_index * group, group, 1)
        right_picks = lax.dynamic_slice_in_dim(picks_b, group_index * group, group, 1)
        left_batch = a_panel[left_picks]
        right_batch = right_ext[right_picks]
        return total + lax.dot_general(
            left_batch,
            right_batch,
            (((1, 3), (1, 2)), ((0,), (0,))),
            preferred_element_type=jnp.float32,
        )

    return lax.fori_loop(0, KP // group, add_group, summed)


def fetch_right(b_blocks, step_index):
    return broadcast(b_blocks, "row", step_index)


def on_device(a_blocks, b_blocks, pair_a, pair_b, owner):
    n_slots = owner.shape[0]
    n_cols = lax.axis_size("col")
    capacity = max(2, 2 * n_slots // n_cols)
    picks_a_all = pair_a.reshape(STEPS, n_slots, KP)
    picks_b_all = pair_b.reshape(STEPS, n_slots, KP)
    group = 4
    summed = jnp.zeros((n_slots, BS, BS), jnp.float32)
    for step_index in range(STEPS):
        a_panel = broadcast(a_blocks, "col", step_index)
        b_panel = fetch_right(b_blocks, step_index)
        summed = step_products(
            a_panel, b_panel, picks_a_all[step_index], picks_b_all[step_index], summed, group
        )
    blocks = summed.astype(jnp.bfloat16)
    owners = owner[:, 0]
    matches = (owners[:, None] == jnp.arange(n_cols, dtype=jnp.int32)[None, :]).astype(jnp.int32)
    order_rank = jnp.sum((jnp.cumsum(matches, axis=0) - matches) * matches, axis=1)
    target = owners * capacity + order_rank
    select = (target[None, :] == jnp.arange(n_cols * capacity, dtype=jnp.int32)[:, None]).astype(
        jnp.bfloat16
    )
    outgoing = jnp.dot(select, blocks.reshape(n_slots, BS * BS), preferred_element_type=jnp.float32)
    outgoing = outgoing.astype(jnp.bfloat16).reshape(n_cols, capacity, BS, BS)
    incoming = lax.all_to_all(outgoing, "col", split_axis=0, concat_axis=0, tiled=True)
    return incoming.reshape(n_cols * capacity, BS, BS)


def solution(mesh):
    return jax.shard_map(
        on_device,
        mesh=mesh,
        in_specs=(
            P("row", "col", None),
            P("row", "col", None),
            P("row", "col"),
            P("row", "col"),
            P(("row", "col"), None),
        ),
        out_specs=P(("row", "col"), None, None),
        check_vma=False,
    )
```

profile of v0, /device:TPU:6, one launch (start us, length us, event | category | flops | bytes accessed | tf_op | source)
XLA Modules:
  0.0 489.6 jit_solution(13857222148430042677)
XLA Ops:
  11.3 212.5 %all-reduce.7.cloned.1.call-done = (bf16[16,128,128]{2,1,0:T(8,128)(2,1)}, bf16[16,128,128]{2,1,0:T(8,128)(2,1)}) async-done(((bf16[16,128,128]{2,1,0:T(8,128)(2,1)}, bf16[16,128,128]{2,1,0:T(8,128)(2,1)}), (bf16[16,128,128]{2,1,0:T(8,128)(2,1)}, bf16[16,128,128]{2,1,0:T(8,128)(2,1)})) %all-reduce.7.cloned.1.call-update) | async-done | bytes 1048592 | tf_op jit(solution)/shard_map/psum | solution.py:13
  226.0 115.0 %all-reduce.9.cloned.1.call-done = (bf16[16,128,128]{2,1,0:T(8,128)(2,1)}, bf16[16,128,128]{2,1,0:T(8,128)(2,1)}) async-done(((bf16[16,128,128]{2,1,0:T(8,128)(2,1)}, bf16[16,128,128]{2,1,0:T(8,128)(2,1)}), (bf16[16,128,128]{2,1,0:T(8,128)(2,1)}, bf16[16,128,128]{2,1,0:T(8,128)(2,1)})) %all-reduce.9.cloned.1.call-update) | async-done | bytes 1048592 | tf_op jit(solution)/shard_map/psum | solution.py:13
  341.0 43.7 %while.28 = (s32[]{:T(128)}, f32[24,128,128]{2,1,0:T(8,128)S(1)}, s32[24,16]{0,1:T(8,128)S(1)}, bf16[16,128,128]{2,1,0:T(8,128)(2,1)}, s32[24,16]{0,1:T(8,128)S(...) while((s32[]{:T(128)}, f32[24,128,128]{2,1,0:T(8,128)S(1)}, ...), condition=%wide.region_5.6_spmd.clone, body=%wide.region_4.5_spmd.clone.sunk | while | flops 403442240 | bytes 22036128 | solution.py:31
  341.2 3.7 gather_fusion.2
  345.1 2.7 gather_fusion.3
  347.9 4.0 bitcast_add_fusion.5
  352.1 3.7 gather_fusion.2
  356.1 2.7 gather_fusion.3
  358.8 4.0 bitcast_add_fusion.5
  363.1 3.7 gather_fusion.2
  367.0 2.7 gather_fusion.3
  369.7 4.0 bitcast_add_fusion.5
  374.0 3.7 gather_fusion.2
  377.9 2.7 gather_fusion.3
  380.7 4.0 bitcast_add_fusion.5
  384.7 39.4 %while.27 = (s32[]{:T(128)}, f32[24,128,128]{2,1,0:T(8,128)S(1)}, s32[24,16]{0,1:T(8,128)S(1)}, bf16[16,128,128]{2,1,0:T(8,128)(2,1)S(1)}, s32[24,16]{0,1:T(8,12...) while((s32[]{:T(128)}, f32[24,128,128]{2,1,0:T(8,128)S(1)}, ...), condition=%wide.region_9.10_spmd, body=%wide.region_8.9_spmd.sunk | while | flops 403049024 | bytes 22036120 | solution.py:31
  387.8 2.7 gather_fusion.1
  390.6 4.0 bitcast_add_fusion.4
  397.7 2.7 gather_fusion.1
  400.4 4.0 bitcast_add_fusion.4
  407.6 2.7 gather_fusion.1
  410.3 4.0 bitcast_add_fusion.4
  420.1 4.0 bitcast_add_fusion.4
  425.4 56.2 %all_to_all.5 = bf16[12,4,128,128]{3,2,1,0:T(8,128)(2,1)S(1)} all-to-all(bf16[12,4,128,128]{3,2,1,0:T(8,128)(2,1)S(1)} %bitcast.49), channel_id=1, replica_groups=mesh['row'=64,'col'=12] {'col'}, dimensions={0} | all-to-all | bytes 3145728 | tf_op jit(solution)/shard_map/all_to_all | solution.py:62
  (103 shorter events, 26.0 us)
Async XLA Ops:
  6.5 4.4 copy-start.3
  6.5 4.7 copy-start.2
  6.5 4.7 copy-start.1
  6.5 217.3 %all-reduce.7.cloned.1.call-start = ((), (), s32[]{:S(2)}) async-start(), calls=%async_computation.1 | async-start | bytes 2097152 | tf_op jit(solution)/shard_map/psum | solution.py:13
  8.7 332.3 %all-reduce.9.cloned.1.call-start = ((), (), s32[]{:S(2)}) async-start(), calls=%async_computation.2 | async-start | bytes 2097152 | tf_op jit(solution)/shard_map/psum | solution.py:13
  341.0 43.7 %copy-start = (bf16[16,128,128]{2,1,0:T(8,128)(2,1)S(1)}, bf16[16,128,128]{2,1,0:T(8,128)(2,1)}, u32[]{:S(2)}) copy-start(bf16[16,128,128]{2,1,0:T(8,128)(2,1)} %get-tuple-element.403) | copy-start | bytes 1572868
Sparse Core Ops, SparseCore 0:
  10.8 212.9 all-reduce.6
  226.4 114.5 all-reduce.8
where the time goes:
time: 490 us
  waiting for transfers between devices  328 us (67%)
  blocking collectives  56.2 us (11%)
  local copies, waits for them, and re-layouts  54.4 us (11%)
  matrix products  32.7 us (7%)
  between operations  13.5 us (3%)
    psum x2, waiting for transfers between devices, broadcast(): return lax.psum(kept, axis)  327 us
    all_to_all x1, blocking collectives, on_device(): lax.all_to_all(outgoing, 'col', split_axis=0, concat_axis=0, tiled=True)  56.2 us
    dot_general x8, matrix products, add_group(): lax.dot_general(left_batch, right_batch, (((1, 3), (1, 2)), ((0,), (0,)))...  31.9 us
    gather x8, local copies, waits for them, and re-layouts, add_group(): left_batch = a_panel[left_picks]  25.7 us
    gather x8, local copies, waits for them, and re-layouts, add_group(): right_batch = right_ext[right_picks]  21.9 us
  transfers between devices with their start and end apart: 2, of which 2 were waited for; matrix products, arithmetic and copies ran while one was open for 1% of the time, Pallas kernels for 0%

commit v1 on v0

v1 whole, which is shorter than its diff:
```python
import functools

import jax
import jax.numpy as jnp
from jax import lax
from jax.experimental import pallas as pl
from jax.experimental.pallas import tpu as pltpu
from jax.sharding import PartitionSpec as P

BS = 128
KP = 16
STEPS = 2
NB = 16
CAP = 4
N_COL = 12
HELD = 3
APART = N_COL // HELD
QUARTER = NB // 4


def signed(hop):
    hop = hop % N_COL
    return hop if hop <= N_COL // 2 else hop - N_COL


def plan_routes():
    chosen, ties = {}, 0
    for apart in range(N_COL):
        options = [(abs(signed(apart + g * APART)), signed(apart + g * APART), g) for g in range(HELD)]
        least = min(o[0] for o in options)
        near = [o for o in options if o[0] == least]
        if len(near) > 1:
            near = [o for o in near if (o[1] > 0) == (ties % 2 == 0)]
            ties += 1
        chosen[apart] = near[0][1:]
    hops = sorted({h for h, _ in chosen.values()}, key=lambda h: (-abs(h), h))
    routes, base, at = {}, {}, 0
    for h in hops:
        routes[h] = sorted(g for hop, g in chosen.values() if hop == h)
        for g in routes[h]:
            apart = (h - g * APART) % N_COL
            base[apart] = (g, at)
            at += CAP
    return routes, base


ROUTES, BASE = plan_routes()
FIRST = {h: sum(CAP * len(v) for k, v in list(ROUTES.items())[: list(ROUTES).index(h)]) for h in ROUTES}


def product_kernel(hops, place, source, picks_a, picks_b, own, from_low, from_high, right_own, right_other, *rest):
    outs, left_all = rest[:-1], rest[-1]
    kind, core = place[0], place[1]

    @pl.when(kind == 0)
    def _():
        left_all[0:NB] = own[...]
        left_all[NB : 2 * NB] = from_high[...]

    @pl.when(kind == 1)
    def _():
        left_all[0:NB] = from_low[...]
        left_all[NB : 2 * NB] = own[...]

    @pl.when(kind == 2)
    def _():
        left_all[0:NB] = from_high[...]
        left_all[NB : 2 * NB] = from_low[...]

    left_all[2 * NB] = jnp.zeros((BS, BS), left_all.dtype)

    def fill(rights):
        for out, hop in zip(outs, hops):

            def one_slot(i, carry, out=out, first=FIRST[hop]):
                at = source[first + i]

                @pl.when(at >= 0)
                def _():
                    total = None
                    for s in range(STEPS):
                        left = [left_all[picks_a[at, s * KP + k]] for k in range(KP)]
                        right = [rights[s][picks_b[at, s * KP + k]] for k in range(KP)]
                        part = jnp.dot(
                            jnp.concatenate(left, 1), jnp.concatenate(right, 0), preferred_element_type=jnp.float32
                        )
                        total = part if total is None else total + part
                    out[i] = total.astype(out.dtype)

                @pl.when(at < 0)
                def _():
                    out[i] = jnp.zeros((BS, BS), out.dtype)

                return carry

            lax.fori_loop(0, out.shape[0], one_slot, 0)

    @pl.when(core == 0)
    def _():
        fill((right_own, right_other))

    @pl.when(core == 1)
    def _():
        fill((right_other, right_own))


def place_kernel(at, *refs):
    arrived, out = refs[:-1], refs[-1]
    for ref, (hop, held) in zip(arrived, ROUTES.items()):
        for n, g in enumerate(held):
            column = lax.rem(at[0] - hop + g * APART + 2 * N_COL, N_COL)
            out[pl.ds(column * CAP, CAP)] = ref[n * CAP : (n + 1) * CAP]


def shift(value, axis, size, hop):
    return lax.ppermute(value, axis, [(i, (i + hop) % size) for i in range(size)])


def x_shift(value, hop):
    return lax.ppermute(
        value, "row", [(8 * y + 2 * x + q, 8 * y + 2 * ((x - hop) % 4) + q) for y in range(8) for x in range(4) for q in range(2)]
    )


def spread_chunk(b_blocks, row):
    got = [
        lax.ppermute(b_blocks[x * QUARTER : (x + 1) * QUARTER], "row", [(0, 2 * x), (1, 2 * x + 1)]) for x in range(1, 4)
    ]
    chunk = b_blocks[0:QUARTER]
    for x in range(1, 4):
        chunk = jnp.where((row // 2) % 4 == x, got[x - 1], chunk)
    y_at = row // 8
    for hops in (((0, 3),), ((0, 5),)), (((0, 1), (3, 4), (5, 6)), ((0, 7), (3, 2))):
        got = [lax.ppermute(chunk, "row", [(8 * a + k, 8 * b + k) for a, b in pairs for k in range(8)]) for pairs in hops]
        for pairs, part in zip(hops, got):
            reached = functools.reduce(jnp.logical_or, [y_at == b for _, b in pairs])
            chunk = jnp.where(reached, part, chunk)
    return chunk


def spread(a_blocks, b_blocks, plan, row, col):
    third = col // 3
    near = lax.ppermute(a_blocks, "col", [(0, 3), (1, 4)])
    far = lax.ppermute(a_blocks, "col", [(0, 9), (1, 10)])
    chunk = spread_chunk(b_blocks, row)
    sent = jnp.concatenate([chunk.reshape(QUARTER * BS, BS), plan], 0)
    came = [shift(sent, "col", N_COL, -g * APART) for g in range(1, HELD)]
    held = jnp.concatenate([chunk] + [c[: QUARTER * BS].reshape(QUARTER, BS, BS) for c in came], 0)
    plans = [plan] + [c[QUARTER * BS :] for c in came]
    own = jnp.where(third == 1, near, jnp.where(third == 3, far, a_blocks))
    held, own = lax.optimization_barrier((held, own))

    after, behind = x_shift(held, 1), x_shift(held, 3)
    half = HELD * QUARTER // 2
    low = lax.ppermute(own[: NB // 2], "col", [(3, 6), (4, 7)])
    high = lax.ppermute(own[NB // 2 :], "col", [(9, 6), (10, 7)])
    own = jnp.where(third == 2, jnp.concatenate([low, high], 0), own)
    after, behind, own = lax.optimization_barrier((after, behind, own))

    across = [x_shift(after[:half], 1), x_shift(behind[half:], 3)]
    from_low = lax.ppermute(own, "col", [(z, (z + 1) % 12) for z in range(12) if z % 3 < 2])
    from_high = lax.ppermute(own, "col", [(z, (z - 1) % 12) for z in range(12) if z % 3 < 2])
    right_own = jnp.concatenate([held, after] + across + [behind], 0)
    right_other = lax.ppermute(right_own, "row", [(i, i ^ 1) for i in range(64)])
    return plans, own, from_low, from_high, right_own, right_other


def on_device(a_blocks, b_blocks, pair_a, pair_b, owner):
    n_slots = owner.shape[0]
    row = lax.axis_index("row")
    col = lax.axis_index("col")
    x_at, core = (row // 2) % 4, row % 2

    plan = jnp.concatenate(
        [pair_a[:n_slots], pair_a[n_slots:], pair_b[:n_slots], pair_b[n_slots:], owner], axis=1
    ).astype(jnp.bfloat16)
    plan = jnp.pad(plan, ((0, 32 - n_slots), (0, BS - plan.shape[1])))
    plans, own, from_low, from_high, right_own, right_other = spread(a_blocks, b_blocks, plan, row, col)
    slots, picks_a, picks_b = [], [], []
    for g, plan in enumerate(plans):
        plan = plan[:n_slots].astype(jnp.int32)
        owners = plan[:, 4 * KP]
        before = jnp.arange(n_slots)[None, :] < jnp.arange(n_slots)[:, None]
        rank = jnp.sum(((owners[:, None] == owners[None, :]) & before).astype(jnp.int32), axis=1)
        apart = (owners - col - g * APART + 2 * N_COL) % N_COL
        start = jnp.full((n_slots,), -N_COL * CAP, jnp.int32)
        for e, (index, at) in BASE.items():
            if index == g:
                start = jnp.where(apart == e, at, start)
        slots.append(start + rank)
        step = (jnp.arange(2 * KP, dtype=jnp.int32) // KP)[None, :]
        block = plan[:, 2 * KP : 4 * KP]
        live = block < NB
        picks_a.append(jnp.where(live, plan[:, : 2 * KP] + step * NB, 2 * NB))
        where = ((block // QUARTER - x_at + 4) % 4) * (HELD * QUARTER) + g * QUARTER + block % QUARTER
        picks_b.append(jnp.where(live, where, 0))
    slots = jnp.concatenate(slots)
    picks_a = jnp.concatenate(picks_a)
    picks_b = jnp.concatenate(picks_b)
    hit = slots[None, :] == jnp.arange(N_COL * CAP, dtype=jnp.int32)[:, None]
    source = jnp.max(jnp.where(hit, jnp.arange(HELD * n_slots, dtype=jnp.int32)[None, :], -1), axis=1)

    smem, vmem = pl.BlockSpec(memory_space=pltpu.SMEM), pl.BlockSpec(memory_space=pltpu.VMEM)

    def products(hops):
        count = sum(CAP * len(ROUTES[h]) for h in hops)
        return pl.pallas_call(
            functools.partial(product_kernel, hops),
            out_shape=[jax.ShapeDtypeStruct((CAP * len(ROUTES[h]), BS, BS), jnp.bfloat16) for h in hops],
            in_specs=[smem] * 4 + [vmem] * 5,
            out_specs=[vmem] * len(hops),
            scratch_shapes=[pltpu.VMEM((2 * NB + 1, BS, BS), jnp.bfloat16)],
            compiler_params=pltpu.CompilerParams(vmem_limit_bytes=24 * 2**20),
            cost_estimate=pl.CostEstimate(flops=count * 2 * KP * BS**3, bytes_accessed=4 * 2**20, transcendentals=0),
            name="products",
        )(jnp.stack([col % 3, core]), source, picks_a, picks_b, own, from_low, from_high, right_own, right_other)

    far = tuple(h for h in ROUTES if h != 0)
    made = list(products(far)) + list(products((0,)))
    arrived = [part if hop == 0 else shift(part, "col", N_COL, hop) for part, hop in zip(made, ROUTES)]
    return pl.pallas_call(
        place_kernel,
        out_shape=jax.ShapeDtypeStruct((N_COL * CAP, BS, BS), jnp.bfloat16),
        in_specs=[smem] + [vmem] * len(ROUTES),
        out_specs=vmem,
        compiler_params=pltpu.CompilerParams(vmem_limit_bytes=16 * 2**20),
        name="arrivals",
    )(jnp.full((1,), col, jnp.int32), *arrived)


def solution(mesh):
    return jax.shard_map(
        on_device,
        mesh=mesh,
        in_specs=(
            P("row", "col", None),
            P("row", "col", None),
            P("row", "col"),
            P("row", "col"),
            P(("row", "col"), None),
        ),
        out_specs=P(("row", "col"), None, None),
        check_vma=False,
    )
```

time: 490 us -> 154 us (0.31)
  the two profiles are of different devices: /device:TPU:6 before, /device:TPU:80 now
where the time goes in v1:
time: 154 us; the launch traced here: 153 us
  starting transfers between devices  69.9 us (45%)
  waiting for transfers between devices  59.6 us (39%)
  Pallas kernels  16.4 us (11%)
  local copies, waits for them, and re-layouts  3.65 us (2%)
  other arithmetic  3.07 us (2%)
    ppermute x6, starting transfers between devices, shift(): lax.ppermute(value, axis, [(i, (i + hop) % size) for i in range(size)])  27.1 us
    ppermute x6, waiting for transfers between devices, shift(): lax.ppermute(value, axis, [(i, (i + hop) % size) for i in range(size)])  19.6 us
    pallas_call x2, Pallas kernels, products(): pl.pallas_call(functools.partial(product_kernel, hops), out_shape=[jax.Sh...  15.1 us
    ppermute x4, starting transfers between devices, x_shift(): lax.ppermute(value, 'row', [(8 * y + 2 * x + q, 8 * y + 2 * ((x - hop) %...  14.2 us
    ppermute x4, waiting for transfers between devices, x_shift(): lax.ppermute(value, 'row', [(8 * y + 2 * x + q, 8 * y + 2 * ((x - hop) %...  13.2 us
    ppermute x4, waiting for transfers between devices, spread_chunk(): lax.ppermute(chunk, 'row', [(8 * a + k, 8 * b + k) for a, b in pairs for...  12.9 us
    ppermute x1, waiting for transfers between devices, spread(): lax.ppermute(own, 'col', [(z, (z - 1) % 12) for z in range(12) if z % 3 <...  9.7 us
    ppermute x1, starting transfers between devices, spread(): near = lax.ppermute(a_blocks, 'col', [(0, 3), (1, 4)])  9.26 us
  transfers between devices with their start and end apart: 24, of which 10 were waited for; matrix products, arithmetic and copies ran while one was open for 4% of the time, Pallas kernels for 2%

profile of v1, /device:TPU:80, one launch (start us, length us, event | category | flops | bytes accessed | tf_op | source)
XLA Modules:
  0.0 153.2 jit_solution(1258766658048550307)
XLA Ops:
  0.0 9.3 %collective-permute-start.9 = (bf16[16,128,128]{2,1,0:T(8,128)(2,1)}, bf16[16,128,128]{2,1,0:T(8,128)(2,1)S(1)}, u32[]{:S(2)}, u32[]{:S(2)}) collective-permute-start(bf16[16,128,128]{2,1,0:T(8,128)(2,1)} %param.5), channel_id=1, source_target_pairs={{0,3},{1,4},{12,15},{13,16},{24,27},{25,28},{36,39},{37,40},{48,51... | collective-permute-start | bytes 1572872 | tf_op jit(solution)/shard_map/ppermute | solution.py:143
  9.3 5.3 %collective-permute-start.10 = (bf16[16,128,128]{2,1,0:T(8,128)(2,1)}, bf16[16,128,128]{2,1,0:T(8,128)(2,1)S(1)}, u32[]{:S(2)}, u32[]{:S(2)}) collective-permute-start(bf16[16,128,128]{2,1,0:T(8,128)(2,1)} %param.5), channel_id=1, source_target_pairs={{0,9},{1,10},{12,21},{13,22},{24,33},{25,34},{36,45},{37,46},{48,5... | collective-permute-start | bytes 1572872 | tf_op jit(solution)/shard_map/ppermute | solution.py:144
  25.2 12.9 %collective-permute-done.5 = bf16[4,128,128]{2,1,0:T(8,128)(2,1)S(1)} collective-permute-done((bf16[4,128,128]{2,1,0:T(8,128)(2,1)S(1)}, bf16[4,128,128]{2,1,0:T(8,128)(2,1)S(1)}, u32[]{:S(2)}, u32[]{:S(2)}) %collective-permute-start.5) | collective-permute-done | bytes 131104 | tf_op jit(solution)/shard_map/ppermute | solution.py:134
  38.1 1.9 %collective-permute-start.8 = (bf16[544,128]{1,0:T(8,128)(2,1)S(1)}, bf16[544,128]{1,0:T(8,128)(2,1)S(1)}, u32[]{:S(2)}, u32[]{:S(2)}) collective-permute-start(bf16[544,128]{1,0:T(8,128)(2,1)S(1)} %pad_maximum_fusion.1), channel_id=1, source_target_pairs={{0,4},{1,5},{2,6},{3,7},{4,8},{5,9},{6,10},{7,11},{8,0},{9,1},{10,... | collective-permute-start | bytes 417800 | tf_op jit(solution)/shard_map/ppermute | solution.py:116
  40.0 7.8 %collective-permute-start.7 = (bf16[544,128]{1,0:T(8,128)(2,1)S(1)}, bf16[544,128]{1,0:T(8,128)(2,1)S(1)}, u32[]{:S(2)}, u32[]{:S(2)}) collective-permute-start(bf16[544,128]{1,0:T(8,128)(2,1)S(1)} %pad_maximum_fusion.1), channel_id=1, source_target_pairs={{0,8},{1,9},{2,10},{3,11},{4,0},{5,1},{6,2},{7,3},{8,4},{9,5},{10,... | collective-permute-start | bytes 417800 | tf_op jit(solution)/shard_map/ppermute | solution.py:116
  48.0 7.1 %collective-permute-done.8 = bf16[544,128]{1,0:T(8,128)(2,1)S(1)} collective-permute-done((bf16[544,128]{1,0:T(8,128)(2,1)S(1)}, bf16[544,128]{1,0:T(8,128)(2,1)S(1)}, u32[]{:S(2)}, u32[]{:S(2)}) %collective-permute-start.8) | collective-permute-done | bytes 139296 | tf_op jit(solution)/shard_map/ppermute | solution.py:116
  55.2 2.7 %collective-permute-start.12 = (bf16[12,128,128]{2,1,0:T(8,128)(2,1)S(1)}, bf16[12,128,128]{2,1,0:T(8,128)(2,1)S(1)}, u32[]{:S(2)}, u32[]{:S(2)}) collective-permute-start(bf16[12,128,128]{2,1,0:T(8,128)(2,1)S(1)} %pad_maximum_fusion), channel_id=1, source_target_pairs={{0,24},{12,36},{24,48},{36,60},{48,72},{60,84},{72,0},{84,12},{96,... | collective-permute-start | bytes 1179656 | tf_op jit(solution)/shard_map/ppermute | solution.py:120
  57.9 4.3 %collective-permute-start.11 = (bf16[12,128,128]{2,1,0:T(8,128)(2,1)S(1)}, bf16[12,128,128]{2,1,0:T(8,128)(2,1)S(1)}, u32[]{:S(2)}, u32[]{:S(2)}) collective-permute-start(bf16[12,128,128]{2,1,0:T(8,128)(2,1)S(1)} %pad_maximum_fusion), channel_id=1, source_target_pairs={{0,72},{12,84},{24,0},{36,12},{48,24},{60,36},{72,48},{84,60},{96,... | collective-permute-start | bytes 1179656 | tf_op jit(solution)/shard_map/ppermute | solution.py:120
  64.4 4.9 %collective-permute-done.12 = bf16[12,128,128]{2,1,0:T(8,128)(2,1)S(1)} collective-permute-done((bf16[12,128,128]{2,1,0:T(8,128)(2,1)S(1)}, bf16[12,128,128]{2,1,0:T(8,128)(2,1)S(1)}, u32[]{:S(2)}, u32[]{:S(2)}) %collective-permute-start.12) | collective-permute-done | bytes 393248 | tf_op jit(solution)/shard_map/ppermute | solution.py:120
  70.9 5.2 %collective-permute-start.17 = (bf16[6,128,128]{2,1,0:T(8,128)(2,1)S(1)}, bf16[6,128,128]{2,1,0:T(8,128)(2,1)S(1)}, u32[]{:S(2)}, u32[]{:S(2)}) collective-permute-start(bf16[6,128,128]{2,1,0:T(8,128)(2,1)S(1)} %slice.110), channel_id=1, source_target_pairs={{0,72},{12,84},{24,0},{36,12},{48,24},{60,36},{72,48},{84,60},{96,... | collective-permute-start | bytes 589832 | tf_op jit(solution)/shard_map/ppermute | solution.py:120
  76.3 1.9 %collective-permute-start.18 = (bf16[6,128,128]{2,1,0:T(8,128)(2,1)S(1)}, bf16[6,128,128]{2,1,0:T(8,128)(2,1)S(1)}, u32[]{:S(2)}, u32[]{:S(2)}) collective-permute-start(bf16[6,128,128]{2,1,0:T(8,128)(2,1)S(1)} %slice.111), channel_id=1, source_target_pairs={{0,24},{12,36},{24,48},{36,60},{48,72},{60,84},{72,0},{84,12},{96,... | collective-permute-start | bytes 589832 | tf_op jit(solution)/shard_map/ppermute | solution.py:120
  79.3 5.8 %collective-permute-done.18 = bf16[6,128,128]{2,1,0:T(8,128)(2,1)S(1)} collective-permute-done((bf16[6,128,128]{2,1,0:T(8,128)(2,1)S(1)}, bf16[6,128,128]{2,1,0:T(8,128)(2,1)S(1)}, u32[]{:S(2)}, u32[]{:S(2)}) %collective-permute-start.18) | collective-permute-done | bytes 196640 | tf_op jit(solution)/shard_map/ppermute | solution.py:120
  85.2 1.9 %collective-permute-start.19 = (bf16[48,128,128]{2,1,0:T(8,128)(2,1)S(1)}, bf16[48,128,128]{2,1,0:T(8,128)(2,1)S(1)}, u32[]{:S(2)}, u32[]{:S(2)}) collective-permute-start(bf16[48,128,128]{2,1,0:T(8,128)(2,1)S(1)} %constant_dynamic-update-slice_fusion.right_own), channel_id=1, source_target_pairs={{0,12},{12,0},{24,36},{36,24},{48,60},{60,48},{72,84},{84,72},{96,... | collective-permute-start | bytes 4718600 | tf_op jit(solution)/shard_map/ppermute | solution.py:164
  87.4 3.6 %collective-permute-start.16 = (bf16[16,128,128]{2,1,0:T(8,128)(2,1)S(1)}, bf16[16,128,128]{2,1,0:T(8,128)(2,1)S(1)}, u32[]{:S(2)}, u32[]{:S(2)}) collective-permute-start(bf16[16,128,128]{2,1,0:T(8,128)(2,1)S(1)} %maximum_select_fusion.own), channel_id=1, source_target_pairs={{0,11},{1,0},{3,2},{4,3},{6,5},{7,6},{9,8},{10,9},{12,23},{13,12},... | collective-permute-start | bytes 1572872 | tf_op jit(solution)/shard_map/ppermute | solution.py:162
  91.0 1.9 %collective-permute-start.15 = (bf16[16,128,128]{2,1,0:T(8,128)(2,1)S(1)}, bf16[16,128,128]{2,1,0:T(8,128)(2,1)S(1)}, u32[]{:S(2)}, u32[]{:S(2)}) collective-permute-start(bf16[16,128,128]{2,1,0:T(8,128)(2,1)S(1)} %maximum_select_fusion.own), channel_id=1, source_target_pairs={{0,1},{1,2},{3,4},{4,5},{6,7},{7,8},{9,10},{10,11},{12,13},{13,14}... | collective-permute-start | bytes 1572872 | tf_op jit(solution)/shard_map/ppermute | solution.py:161
  93.1 9.7 %collective-permute-done.16.from_high = bf16[16,128,128]{2,1,0:T(8,128)(2,1)S(1)} collective-permute-done((bf16[16,128,128]{2,1,0:T(8,128)(2,1)S(1)}, bf16[16,128,128]{2,1,0:T(8,128)(2,1)S(1)}, u32[]{:S(2)}, u32[]{:S(2)}) %collective-permute-start.16) | collective-permute-done | bytes 524320 | tf_op jit(solution)/shard_map/ppermute | solution.py:162
  102.8 4.1 %collective-permute-done.15.from_low = bf16[16,128,128]{2,1,0:T(8,128)(2,1)S(1)} collective-permute-done((bf16[16,128,128]{2,1,0:T(8,128)(2,1)S(1)}, bf16[16,128,128]{2,1,0:T(8,128)(2,1)S(1)}, u32[]{:S(2)}, u32[]{:S(2)}) %collective-permute-start.15) | collective-permute-done | bytes 524320 | tf_op jit(solution)/shard_map/ppermute | solution.py:161
  107.0 11.8 %products.2 = (bf16[4,128,128]{2,1,0:T(8,128)(2,1)S(1)}, bf16[8,128,128]{2,1,0:T(8,128)(2,1)S(1)}, bf16[12,128,128]{2,1,0:T(8,128)(2,1)S(1)}, bf16[12,128,128]{2,1,0:T(8,128)(2,1)S(1)}) custom-call(s32[2]{0:T(128)S(1)} %pad_add_fusion.2.place, s32[48]{0:T(128)S(1)} %select_reduce_fusion.source, s32[72,32]{1,0:T(8,128)S(1)} %pad_add_fusion.picks_a, ...), custom_call_target="tpu_custom_call" | custom-call | flops 2415919104 | bytes 4194304 | tf_op jit(solution)/shard_map/products/pallas_call | solution.py:207
  118.8 1.9 %collective-permute-start.22 = (bf16[12,128,128]{2,1,0:T(8,128)(2,1)S(1)}, bf16[12,128,128]{2,1,0:T(8,128)(2,1)S(1)}, u32[]{:S(2)}, u32[]{:S(2)}) collective-permute-start(bf16[12,128,128]{2,1,0:T(8,128)(2,1)S(1)} %get-tuple-element.21), channel_id=1, source_target_pairs={{0,11},{1,0},{2,1},{3,2},{4,3},{5,4},{6,5},{7,6},{8,7},{9,8},{10,9... | collective-permute-start | bytes 1179656 | tf_op jit(solution)/shard_map/ppermute | solution.py:116
  120.7 3.9 %collective-permute-start.23 = (bf16[12,128,128]{2,1,0:T(8,128)(2,1)S(1)}, bf16[12,128,128]{2,1,0:T(8,128)(2,1)S(1)}, u32[]{:S(2)}, u32[]{:S(2)}) collective-permute-start(bf16[12,128,128]{2,1,0:T(8,128)(2,1)S(1)} %get-tuple-element.22), channel_id=1, source_target_pairs={{0,1},{1,2},{2,3},{3,4},{4,5},{5,6},{6,7},{7,8},{8,9},{9,10},{10,1... | collective-permute-start | bytes 1179656 | tf_op jit(solution)/shard_map/ppermute | solution.py:116
  124.6 3.4 %collective-permute-start.21 = (bf16[8,128,128]{2,1,0:T(8,128)(2,1)S(1)}, bf16[8,128,128]{2,1,0:T(8,128)(2,1)S(1)}, u32[]{:S(2)}, u32[]{:S(2)}) collective-permute-start(bf16[8,128,128]{2,1,0:T(8,128)(2,1)S(1)} %get-tuple-element.20), channel_id=1, source_target_pairs={{0,2},{1,3},{2,4},{3,5},{4,6},{5,7},{6,8},{7,9},{8,10},{9,11},{10,... | collective-permute-start | bytes 786440 | tf_op jit(solution)/shard_map/ppermute | solution.py:116
  128.1 8.1 %collective-permute-start.20 = (bf16[4,128,128]{2,1,0:T(8,128)(2,1)S(1)}, bf16[4,128,128]{2,1,0:T(8,128)(2,1)S(1)}, u32[]{:S(2)}, u32[]{:S(2)}) collective-permute-start(bf16[4,128,128]{2,1,0:T(8,128)(2,1)S(1)} %get-tuple-element.19), channel_id=1, source_target_pairs={{0,10},{1,11},{2,0},{3,1},{4,2},{5,3},{6,4},{7,5},{8,6},{9,7},{10,... | collective-permute-start | bytes 393224 | tf_op jit(solution)/shard_map/ppermute | solution.py:116
  136.2 3.3 %products.3.refs_4_ = bf16[12,128,128]{2,1,0:T(8,128)(2,1)S(1)} custom-call(s32[2]{0:T(128)S(1)} %pad_add_fusion.2.place, s32[48]{0:T(128)S(1)} %select_reduce_fusion.source, s32[72,32]{1,0:T(8,128)S(1)} %pad_add_fusion.picks_a, s32[72,32]{1,0:T(8,128)S(1)} %pad_add_fusion.1.picks_b, bf16[16,128,128]{2,1,0:T(8,128)(2,1)S(1)} %maximum_select_fusion.own, ...), custom_call_target="tpu_custom_call" | custom-call | flops 805306368 | bytes 4194304 | tf_op jit(solution)/shard_map/products/pallas_call | solution.py:207
  141.3 10.7 %collective-permute-done.21.refs_1_ = bf16[8,128,128]{2,1,0:T(8,128)(2,1)S(1)} collective-permute-done((bf16[8,128,128]{2,1,0:T(8,128)(2,1)S(1)}, bf16[8,128,128]{2,1,0:T(8,128)(2,1)S(1)}, u32[]{:S(2)}, u32[]{:S(2)}) %collective-permute-start.21) | collective-permute-done | bytes 262176 | tf_op jit(solution)/shard_map/ppermute | solution.py:116
  (78 shorter events, 19.0 us)
Async XLA Ops:
  0.0 47.8 %collective-permute-start.9 = (bf16[16,128,128]{2,1,0:T(8,128)(2,1)}, bf16[16,128,128]{2,1,0:T(8,128)(2,1)S(1)}, u32[]{:S(2)}, u32[]{:S(2)}) collective-permute-start(bf16[16,128,128]{2,1,0:T(8,128)(2,1)} %param.5), channel_id=1, source_target_pairs={{0,3},{1,4},{12,15},{13,16},{24,27},{25,28},{36,39},{37,40},{48,51... | collective-permute-start | bytes 1572872 | tf_op jit(solution)/shard_map/ppermute | solution.py:143
  9.3 38.6 %collective-permute-start.10 = (bf16[16,128,128]{2,1,0:T(8,128)(2,1)}, bf16[16,128,128]{2,1,0:T(8,128)(2,1)S(1)}, u32[]{:S(2)}, u32[]{:S(2)}) collective-permute-start(bf16[16,128,128]{2,1,0:T(8,128)(2,1)} %param.5), channel_id=1, source_target_pairs={{0,9},{1,10},{12,21},{13,22},{24,33},{25,34},{36,45},{37,46},{48,5... | collective-permute-start | bytes 1572872 | tf_op jit(solution)/shard_map/ppermute | solution.py:144
  15.6 5.0 %collective-permute-start.2 = (bf16[4,128,128]{2,1,0:T(8,128)(2,1)S(1)}, bf16[4,128,128]{2,1,0:T(8,128)(2,1)S(1)}, u32[]{:S(2)}, u32[]{:S(2)}) collective-permute-start(bf16[4,128,128]{2,1,0:T(8,128)(2,1)S(1)} %get-tuple-element.31), channel_id=1, source_target_pairs={{0,24},{12,36},{1,25},{13,37},{2,26},{14,38},{3,27},{15,39},{4,28}... | collective-permute-start | bytes 393224 | tf_op jit(solution)/shard_map/ppermute | solution.py:127
  16.3 4.3 %collective-permute-start.1 = (bf16[4,128,128]{2,1,0:T(8,128)(2,1)S(1)}, bf16[4,128,128]{2,1,0:T(8,128)(2,1)S(1)}, u32[]{:S(2)}, u32[]{:S(2)}) collective-permute-start(bf16[4,128,128]{2,1,0:T(8,128)(2,1)S(1)} %get-tuple-element.32), channel_id=1, source_target_pairs={{0,48},{12,60},{1,49},{13,61},{2,50},{14,62},{3,51},{15,63},{4,52}... | collective-permute-start | bytes 393224 | tf_op jit(solution)/shard_map/ppermute | solution.py:127
  16.9 3.7 %collective-permute-start = (bf16[4,128,128]{2,1,0:T(8,128)(2,1)S(1)}, bf16[4,128,128]{2,1,0:T(8,128)(2,1)S(1)}, u32[]{:S(2)}, u32[]{:S(2)}) collective-permute-start(bf16[4,128,128]{2,1,0:T(8,128)(2,1)S(1)} %get-tuple-element.33), channel_id=1, source_target_pairs={{0,72},{12,84},{1,73},{13,85},{2,74},{14,86},{3,75},{15,87},{4,76}... | collective-permute-start | bytes 393224 | tf_op jit(solution)/shard_map/ppermute | solution.py:127
  21.6 1.4 collective-permute-start.4
  22.2 0.7 collective-permute-start.3
  23.0 2.2 %collective-permute-start.6 = (bf16[4,128,128]{2,1,0:T(8,128)(2,1)S(1)}, bf16[4,128,128]{2,1,0:T(8,128)(2,1)S(1)}, u32[]{:S(2)}, u32[]{:S(2)}) collective-permute-start(bf16[4,128,128]{2,1,0:T(8,128)(2,1)S(1)} %select_select_fusion.2), channel_id=1, source_target_pairs={{0,96},{12,108},{24,120},{36,132},{48,144},{60,156},{72,168},{84,1... | collective-permute-start | bytes 393224 | tf_op jit(solution)/shard_map/ppermute | solution.py:134
  23.7 14.4 %collective-permute-start.5 = (bf16[4,128,128]{2,1,0:T(8,128)(2,1)S(1)}, bf16[4,128,128]{2,1,0:T(8,128)(2,1)S(1)}, u32[]{:S(2)}, u32[]{:S(2)}) collective-permute-start(bf16[4,128,128]{2,1,0:T(8,128)(2,1)S(1)} %select_select_fusion.2), channel_id=1, source_target_pairs={{0,672},{12,684},{24,696},{36,708},{48,720},{60,732},{72,744},{84,... | collective-permute-start | bytes 393224 | tf_op jit(solution)/shard_map/ppermute | solution.py:134
  38.1 17.0 %collective-permute-start.8 = (bf16[544,128]{1,0:T(8,128)(2,1)S(1)}, bf16[544,128]{1,0:T(8,128)(2,1)S(1)}, u32[]{:S(2)}, u32[]{:S(2)}) collective-permute-start(bf16[544,128]{1,0:T(8,128)(2,1)S(1)} %pad_maximum_fusion.1), channel_id=1, source_target_pairs={{0,4},{1,5},{2,6},{3,7},{4,8},{5,9},{6,10},{7,11},{8,0},{9,1},{10,... | collective-permute-start | bytes 417800 | tf_op jit(solution)/shard_map/ppermute | solution.py:116
  40.0 15.1 %collective-permute-start.7 = (bf16[544,128]{1,0:T(8,128)(2,1)S(1)}, bf16[544,128]{1,0:T(8,128)(2,1)S(1)}, u32[]{:S(2)}, u32[]{:S(2)}) collective-permute-start(bf16[544,128]{1,0:T(8,128)(2,1)S(1)} %pad_maximum_fusion.1), channel_id=1, source_target_pairs={{0,8},{1,9},{2,10},{3,11},{4,0},{5,1},{6,2},{7,3},{8,4},{9,5},{10,... | collective-permute-start | bytes 417800 | tf_op jit(solution)/shard_map/ppermute | solution.py:116
  55.2 14.1 %collective-permute-start.12 = (bf16[12,128,128]{2,1,0:T(8,128)(2,1)S(1)}, bf16[12,128,128]{2,1,0:T(8,128)(2,1)S(1)}, u32[]{:S(2)}, u32[]{:S(2)}) collective-permute-start(bf16[12,128,128]{2,1,0:T(8,128)(2,1)S(1)} %pad_maximum_fusion), channel_id=1, source_target_pairs={{0,24},{12,36},{24,48},{36,60},{48,72},{60,84},{72,0},{84,12},{96,... | collective-permute-start | bytes 1179656 | tf_op jit(solution)/shard_map/ppermute | solution.py:120
  57.9 12.9 %collective-permute-start.11 = (bf16[12,128,128]{2,1,0:T(8,128)(2,1)S(1)}, bf16[12,128,128]{2,1,0:T(8,128)(2,1)S(1)}, u32[]{:S(2)}, u32[]{:S(2)}) collective-permute-start(bf16[12,128,128]{2,1,0:T(8,128)(2,1)S(1)} %pad_maximum_fusion), channel_id=1, source_target_pairs={{0,72},{12,84},{24,0},{36,12},{48,24},{60,36},{72,48},{84,60},{96,... | collective-permute-start | bytes 1179656 | tf_op jit(solution)/shard_map/ppermute | solution.py:120
  62.5 1.8 %collective-permute-start.13 = (bf16[8,128,128]{2,1,0:T(8,128)(2,1)S(1)}, bf16[8,128,128]{2,1,0:T(8,128)(2,1)S(1)}, u32[]{:S(2)}, u32[]{:S(2)}) collective-permute-start(bf16[8,128,128]{2,1,0:T(8,128)(2,1)S(1)} %get-tuple-element.29), channel_id=1, source_target_pairs={{3,6},{4,7},{15,18},{16,19},{27,30},{28,31},{39,42},{40,43},{51,54... | collective-permute-start | bytes 786440 | tf_op jit(solution)/shard_map/ppermute | solution.py:155
  63.2 1.1 collective-permute-start.14
  70.9 8.4 %collective-permute-start.17 = (bf16[6,128,128]{2,1,0:T(8,128)(2,1)S(1)}, bf16[6,128,128]{2,1,0:T(8,128)(2,1)S(1)}, u32[]{:S(2)}, u32[]{:S(2)}) collective-permute-start(bf16[6,128,128]{2,1,0:T(8,128)(2,1)S(1)} %slice.110), channel_id=1, source_target_pairs={{0,72},{12,84},{24,0},{36,12},{48,24},{60,36},{72,48},{84,60},{96,... | collective-permute-start | bytes 589832 | tf_op jit(solution)/shard_map/ppermute | solution.py:120
  76.3 8.8 %collective-permute-start.18 = (bf16[6,128,128]{2,1,0:T(8,128)(2,1)S(1)}, bf16[6,128,128]{2,1,0:T(8,128)(2,1)S(1)}, u32[]{:S(2)}, u32[]{:S(2)}) collective-permute-start(bf16[6,128,128]{2,1,0:T(8,128)(2,1)S(1)} %slice.111), channel_id=1, source_target_pairs={{0,24},{12,36},{24,48},{36,60},{48,72},{60,84},{72,0},{84,12},{96,... | collective-permute-start | bytes 589832 | tf_op jit(solution)/shard_map/ppermute | solution.py:120
  85.2 21.8 %collective-permute-start.19 = (bf16[48,128,128]{2,1,0:T(8,128)(2,1)S(1)}, bf16[48,128,128]{2,1,0:T(8,128)(2,1)S(1)}, u32[]{:S(2)}, u32[]{:S(2)}) collective-permute-start(bf16[48,128,128]{2,1,0:T(8,128)(2,1)S(1)} %constant_dynamic-update-slice_fusion.right_own), channel_id=1, source_target_pairs={{0,12},{12,0},{24,36},{36,24},{48,60},{60,48},{72,84},{84,72},{96,... | collective-permute-start | bytes 4718600 | tf_op jit(solution)/shard_map/ppermute | solution.py:164
  87.4 15.4 %collective-permute-start.16 = (bf16[16,128,128]{2,1,0:T(8,128)(2,1)S(1)}, bf16[16,128,128]{2,1,0:T(8,128)(2,1)S(1)}, u32[]{:S(2)}, u32[]{:S(2)}) collective-permute-start(bf16[16,128,128]{2,1,0:T(8,128)(2,1)S(1)} %maximum_select_fusion.own), channel_id=1, source_target_pairs={{0,11},{1,0},{3,2},{4,3},{6,5},{7,6},{9,8},{10,9},{12,23},{13,12},... | collective-permute-start | bytes 1572872 | tf_op jit(solution)/shard_map/ppermute | solution.py:162
  91.0 15.9 %collective-permute-start.15 = (bf16[16,128,128]{2,1,0:T(8,128)(2,1)S(1)}, bf16[16,128,128]{2,1,0:T(8,128)(2,1)S(1)}, u32[]{:S(2)}, u32[]{:S(2)}) collective-permute-start(bf16[16,128,128]{2,1,0:T(8,128)(2,1)S(1)} %maximum_select_fusion.own), channel_id=1, source_target_pairs={{0,1},{1,2},{3,4},{4,5},{6,7},{7,8},{9,10},{10,11},{12,13},{13,14}... | collective-permute-start | bytes 1572872 | tf_op jit(solution)/shard_map/ppermute | solution.py:161
  118.8 33.2 %collective-permute-start.22 = (bf16[12,128,128]{2,1,0:T(8,128)(2,1)S(1)}, bf16[12,128,128]{2,1,0:T(8,128)(2,1)S(1)}, u32[]{:S(2)}, u32[]{:S(2)}) collective-permute-start(bf16[12,128,128]{2,1,0:T(8,128)(2,1)S(1)} %get-tuple-element.21), channel_id=1, source_target_pairs={{0,11},{1,0},{2,1},{3,2},{4,3},{5,4},{6,5},{7,6},{8,7},{9,8},{10,9... | collective-permute-start | bytes 1179656 | tf_op jit(solution)/shard_map/ppermute | solution.py:116
  120.7 31.2 %collective-permute-start.23 = (bf16[12,128,128]{2,1,0:T(8,128)(2,1)S(1)}, bf16[12,128,128]{2,1,0:T(8,128)(2,1)S(1)}, u32[]{:S(2)}, u32[]{:S(2)}) collective-permute-start(bf16[12,128,128]{2,1,0:T(8,128)(2,1)S(1)} %get-tuple-element.22), channel_id=1, source_target_pairs={{0,1},{1,2},{2,3},{3,4},{4,5},{5,6},{6,7},{7,8},{8,9},{9,10},{10,1... | collective-permute-start | bytes 1179656 | tf_op jit(solution)/shard_map/ppermute | solution.py:116
  124.6 27.3 %collective-permute-start.21 = (bf16[8,128,128]{2,1,0:T(8,128)(2,1)S(1)}, bf16[8,128,128]{2,1,0:T(8,128)(2,1)S(1)}, u32[]{:S(2)}, u32[]{:S(2)}) collective-permute-start(bf16[8,128,128]{2,1,0:T(8,128)(2,1)S(1)} %get-tuple-element.20), channel_id=1, source_target_pairs={{0,2},{1,3},{2,4},{3,5},{4,6},{5,7},{6,8},{7,9},{8,10},{9,11},{10,... | collective-permute-start | bytes 786440 | tf_op jit(solution)/shard_map/ppermute | solution.py:116
  128.1 13.2 %collective-permute-start.20 = (bf16[4,128,128]{2,1,0:T(8,128)(2,1)S(1)}, bf16[4,128,128]{2,1,0:T(8,128)(2,1)S(1)}, u32[]{:S(2)}, u32[]{:S(2)}) collective-permute-start(bf16[4,128,128]{2,1,0:T(8,128)(2,1)S(1)} %get-tuple-element.19), channel_id=1, source_target_pairs={{0,10},{1,11},{2,0},{3,1},{4,2},{5,3},{6,4},{7,5},{8,6},{9,7},{10,... | collective-permute-start | bytes 393224 | tf_op jit(solution)/shard_map/ppermute | solution.py:116
  (1 other events, 47.9 us)

commit v2 on v1

--- a/solution.py
+++ b/solution.py
@@ -16,6 +16,8 @@
 HELD = 3
 APART = N_COL // HELD
 QUARTER = NB // 4
+SLOTS = 24
+TOGETHER = 3
 
 
 def signed(hop):
@@ -48,9 +50,10 @@
 FIRST = {h: sum(CAP * len(v) for k, v in list(ROUTES.items())[: list(ROUTES).index(h)]) for h in ROUTES}
 
 
-def product_kernel(hops, place, source, picks_a, picks_b, own, from_low, from_high, right_own, right_other, *rest):
+def product_kernel(hops, table, own, from_low, from_high, right_own, right_other, *rest):
     outs, left_all = rest[:-1], rest[-1]
-    kind, core = place[0], place[1]
+    notes = HELD * SLOTS
+    kind, core = table[notes, 0], table[notes, 1]
 
     @pl.when(kind == 0)
     def _():
@@ -69,31 +72,29 @@
 
     left_all[2 * NB] = jnp.zeros((BS, BS), left_all.dtype)
 
+    def one_block(rights, at):
+        total = None
+        for s in range(STEPS):
+            left = [left_all[table[at, s * KP + k]] for k in range(KP)]
+            right = [rights[s][table[at, (STEPS + s) * KP + k]] for k in range(KP)]
+            part = jnp.dot(jnp.concatenate(left, 1), jnp.concatenate(right, 0), preferred_element_type=jnp.float32)
+            total = part if total is None else total + part
+        return total
+
     def fill(rights):
         for out, hop in zip(outs, hops):
 
-            def one_slot(i, carry, out=out, first=FIRST[hop]):
-                at = source[first + i]
-
-                @pl.when(at >= 0)
-                def _():
-                    total = None
-                    for s in range(STEPS):
-                        left = [left_all[picks_a[at, s * KP + k]] for k in range(KP)]
-                        right = [rights[s][picks_b[at, s * KP + k]] for k in range(KP)]
-                        part = jnp.dot(
-                            jnp.concatenate(left, 1), jnp.concatenate(right, 0), preferred_element_type=jnp.float32
-                        )
-                        total = part if total is None else total + part
-                    out[i] = total.astype(out.dtype)
-
-                @pl.when(at < 0)
-                def _():
-                    out[i] = jnp.zeros((BS, BS), out.dtype)
-
+            number, first = table[notes, 2 + list(ROUTES).index(hop)], FIRST[hop]
+            out[...] = jnp.zeros_like(out)
+
+            def some_slots(i, carry, out=out, number=number, first=first):
+                places = [first + jnp.minimum(TOGETHER * i + u, number - 1) for u in range(TOGETHER)]
+                sums = [one_block(rights, table[notes + 2, p]) for p in places]
+                for p, total in zip(places, sums):
+                    out[table[notes + 1, p]] = total.astype(out.dtype)
                 return carry
 
-            lax.fori_loop(0, out.shape[0], one_slot, 0)
+            lax.fori_loop(0, (number + TOGETHER - 1) // TOGETHER, some_slots, 0)
 
     @pl.when(core == 0)
     def _():
@@ -112,6 +113,17 @@
             out[pl.ds(column * CAP, CAP)] = ref[n * CAP : (n + 1) * CAP]
 
 
+def join_kernel(third, own, low, high, out):
+    @pl.when(third[0] == 2)
+    def _():
+        out[0 : NB // 2] = low[...]
+        out[NB // 2 :] = high[...]
+
+    @pl.when(third[0] != 2)
+    def _():
+        out[...] = own[...]
+
+
 def shift(value, axis, size, hop):
     return lax.ppermute(value, axis, [(i, (i + hop) % size) for i in range(size)])
 
@@ -122,11 +134,9 @@
     )
 
 
-def spread_chunk(b_blocks, row):
-    got = [
-        lax.ppermute(b_blocks[x * QUARTER : (x + 1) * QUARTER], "row", [(0, 2 * x), (1, 2 * x + 1)]) for x in range(1, 4)
-    ]
-    chunk = b_blocks[0:QUARTER]
+def spread_chunk(quarters, row):
+    got = [lax.ppermute(quarters[x], "row", [(0, 2 * x), (1, 2 * x + 1)]) for x in range(1, 4)]
+    chunk = quarters[0]
     for x in range(1, 4):
         chunk = jnp.where((row // 2) % 4 == x, got[x - 1], chunk)
     y_at = row // 8
@@ -140,27 +150,35 @@
 
 def spread(a_blocks, b_blocks, plan, row, col):
     third = col // 3
+    quarters = [b_blocks[x * QUARTER : (x + 1) * QUARTER] for x in range(4)]
     near = lax.ppermute(a_blocks, "col", [(0, 3), (1, 4)])
     far = lax.ppermute(a_blocks, "col", [(0, 9), (1, 10)])
-    chunk = spread_chunk(b_blocks, row)
+    chunk = spread_chunk(quarters, row)
     sent = jnp.concatenate([chunk.reshape(QUARTER * BS, BS), plan], 0)
     came = [shift(sent, "col", N_COL, -g * APART) for g in range(1, HELD)]
     held = jnp.concatenate([chunk] + [c[: QUARTER * BS].reshape(QUARTER, BS, BS) for c in came], 0)
     plans = [plan] + [c[QUARTER * BS :] for c in came]
     own = jnp.where(third == 1, near, jnp.where(third == 3, far, a_blocks))
-    held, own = lax.optimization_barrier((held, own))
-
-    after, behind = x_shift(held, 1), x_shift(held, 3)
-    half = HELD * QUARTER // 2
     low = lax.ppermute(own[: NB // 2], "col", [(3, 6), (4, 7)])
     high = lax.ppermute(own[NB // 2 :], "col", [(9, 6), (10, 7)])
-    own = jnp.where(third == 2, jnp.concatenate([low, high], 0), own)
+    own = pl.pallas_call(
+        join_kernel,
+        out_shape=jax.ShapeDtypeStruct(own.shape, own.dtype),
+        in_specs=[pl.BlockSpec(memory_space=pltpu.SMEM)] + [pl.BlockSpec(memory_space=pltpu.VMEM)] * 3,
+        out_specs=pl.BlockSpec(memory_space=pltpu.VMEM),
+        compiler_params=pltpu.CompilerParams(vmem_limit_bytes=8 * 2**20),
+        cost_estimate=pl.CostEstimate(flops=10**10, bytes_accessed=2**20, transcendentals=0),
+        name="join",
+    )(jnp.full((1,), third, jnp.int32), own, low, high)
+
+    after, behind = x_shift(held, 1), x_shift(held, 3)
     after, behind, own = lax.optimization_barrier((after, behind, own))
-
-    across = [x_shift(after[:half], 1), x_shift(behind[half:], 3)]
+    half = HELD * QUARTER // 2
     from_low = lax.ppermute(own, "col", [(z, (z + 1) % 12) for z in range(12) if z % 3 < 2])
     from_high = lax.ppermute(own, "col", [(z, (z - 1) % 12) for z in range(12) if z % 3 < 2])
+    across = [x_shift(after[:half], 1), x_shift(behind[half:], 3)]
     right_own = jnp.concatenate([held, after] + across + [behind], 0)
+    right_own, from_low, from_high = lax.optimization_barrier((right_own, from_low, from_high))
     right_other = lax.ppermute(right_own, "row", [(i, i ^ 1) for i in range(64)])
     return plans, own, from_low, from_high, right_own, right_other
 
@@ -176,7 +194,7 @@
     ).astype(jnp.bfloat16)
     plan = jnp.pad(plan, ((0, 32 - n_slots), (0, BS - plan.shape[1])))
     plans, own, from_low, from_high, right_own, right_other = spread(a_blocks, b_blocks, plan, row, col)
-    slots, picks_a, picks_b = [], [], []
+    slots, picks = [], []
     for g, plan in enumerate(plans):
         plan = plan[:n_slots].astype(jnp.int32)
         owners = plan[:, 4 * KP]
@@ -191,14 +209,26 @@
         step = (jnp.arange(2 * KP, dtype=jnp.int32) // KP)[None, :]
         block = plan[:, 2 * KP : 4 * KP]
         live = block < NB
-        picks_a.append(jnp.where(live, plan[:, : 2 * KP] + step * NB, 2 * NB))
+        left = jnp.where(live, plan[:, : 2 * KP] + step * NB, 2 * NB)
         where = ((block // QUARTER - x_at + 4) % 4) * (HELD * QUARTER) + g * QUARTER + block % QUARTER
-        picks_b.append(jnp.where(live, where, 0))
+        picks.append(jnp.concatenate([left, jnp.where(live, where, 0)], 1))
     slots = jnp.concatenate(slots)
-    picks_a = jnp.concatenate(picks_a)
-    picks_b = jnp.concatenate(picks_b)
     hit = slots[None, :] == jnp.arange(N_COL * CAP, dtype=jnp.int32)[:, None]
     source = jnp.max(jnp.where(hit, jnp.arange(HELD * n_slots, dtype=jnp.int32)[None, :], -1), axis=1)
+    group = jnp.concatenate([jnp.full((CAP * len(ROUTES[h]),), n, jnp.int32) for n, h in enumerate(ROUTES)])
+    base = jnp.concatenate([jnp.full((CAP * len(ROUTES[h]),), FIRST[h], jnp.int32) for h in ROUTES])
+    index = jnp.arange(N_COL * CAP, dtype=jnp.int32)
+    filled = source >= 0
+    ahead = (group[:, None] == group[None, :]) & (index[None, :] < index[:, None]) & filled[None, :]
+    position = base + jnp.sum(ahead.astype(jnp.int32), axis=1)
+    named = (position[None, :] == index[:, None]) & filled[None, :]
+    slot_of = jnp.sum(jnp.where(named, (index - base)[None, :], 0), axis=1)
+    row_of = jnp.sum(jnp.where(named, source[None, :], 0), axis=1)
+    here = (group[None, :] == jnp.arange(len(ROUTES), dtype=jnp.int32)[:, None]) & filled[None, :]
+    counts = jnp.sum(here.astype(jnp.int32), axis=1)
+    notes = [jnp.concatenate([jnp.stack([col % 3, core]), counts]), slot_of, row_of]
+    notes = jnp.stack([jnp.pad(n, (0, BS - n.shape[0])) for n in notes])
+    table = jnp.concatenate([jnp.pad(jnp.concatenate(picks), ((0, 0), (0, BS - 4 * KP))), notes])
 
     smem, vmem = pl.BlockSpec(memory_space=pltpu.SMEM), pl.BlockSpec(memory_space=pltpu.VMEM)
 
@@ -207,16 +237,17 @@
         return pl.pallas_call(
             functools.partial(product_kernel, hops),
             out_shape=[jax.ShapeDtypeStruct((CAP * len(ROUTES[h]), BS, BS), jnp.bfloat16) for h in hops],
-            in_specs=[smem] * 4 + [vmem] * 5,
+            in_specs=[smem] + [vmem] * 5,
             out_specs=[vmem] * len(hops),
             scratch_shapes=[pltpu.VMEM((2 * NB + 1, BS, BS), jnp.bfloat16)],
             compiler_params=pltpu.CompilerParams(vmem_limit_bytes=24 * 2**20),
             cost_estimate=pl.CostEstimate(flops=count * 2 * KP * BS**3, bytes_accessed=4 * 2**20, transcendentals=0),
             name="products",
-        )(jnp.stack([col % 3, core]), source, picks_a, picks_b, own, from_low, from_high, right_own, right_other)
-
-    far = tuple(h for h in ROUTES if h != 0)
-    made = list(products(far)) + list(products((0,)))
+        )(table, own, from_low, from_high, right_own, right_other)
+
+    made = []
+    for distance in sorted({abs(h) for h in ROUTES}, reverse=True):
+        made += products(tuple(h for h in ROUTES if abs(h) == distance))
     arrived = [part if hop == 0 else shift(part, "col", N_COL, hop) for part, hop in zip(made, ROUTES)]
     return pl.pallas_call(
         place_kernel,

time: 154 us -> 135 us (0.88)
  waiting for transfers between devices: 59.6 us -> 44.2 us
  Pallas kernels: 16.4 us -> 13.8 us
  starting transfers between devices: 69.9 us -> 68.3 us
    ppermute x1, waiting for transfers between devices: 9.7 us -> 0.01 us  [spread(): lax.ppermute(own, 'col', [(z, (z - 1) % 12) for z in range(12) if z % 3 <...]
    ppermute x6, waiting for transfers between devices: 19.6 us -> 14.1 us  [shift(): lax.ppermute(value, axis, [(i, (i + hop) % size) for i in range(size)])]
    ppermute x1, waiting for transfers between devices: 4.15 us -> 0.01 us  [spread(): lax.ppermute(own, 'col', [(z, (z + 1) % 12) for z in range(12) if z % 3 <...]
    pallas_call x2 -> x3, Pallas kernels: 15.1 us -> 12.4 us  [products(): pl.pallas_call(functools.partial(product_kernel, hops), out_shape=[jax.Sh...]
    ppermute x1, waiting for transfers between devices: 0.01 us -> 2.63 us  [spread(): lax.ppermute(right_own, 'row', [(i, i ^ 1) for i in range(64)])]
    ppermute x4, waiting for transfers between devices: 13.2 us -> 14.9 us  [x_shift(): lax.ppermute(value, 'row', [(8 * y + 2 * x + q, 8 * y + 2 * ((x - hop) %...]
  transfers between devices with their start and end apart: 24 -> 24, of which waited for: 10 -> 8; matrix products, arithmetic and copies ran while one was open for 4% -> 5% of each run, Pallas kernels for 2% -> 6%
where the time goes in v2:
time: 135 us; the launch traced here: 134 us
  starting transfers between devices  68.3 us (51%)
  waiting for transfers between devices  44.2 us (33%)
  Pallas kernels  13.8 us (10%)
  local copies, waits for them, and re-layouts  3.69 us (3%)
  other arithmetic  3.51 us (3%)
    ppermute x6, starting transfers between devices, shift(): lax.ppermute(value, axis, [(i, (i + hop) % size) for i in range(size)])  26.8 us
    ppermute x4, waiting for transfers between devices, x_shift(): lax.ppermute(value, 'row', [(8 * y + 2 * x + q, 8 * y + 2 * ((x - hop) %...  14.9 us
    ppermute x6, waiting for transfers between devices, shift(): lax.ppermute(value, axis, [(i, (i + hop) % size) for i in range(size)])  14.1 us
    ppermute x4, starting transfers between devices, x_shift(): lax.ppermute(value, 'row', [(8 * y + 2 * x + q, 8 * y + 2 * ((x - hop) %...  13.3 us
    ppermute x4, waiting for transfers between devices, spread_chunk(): lax.ppermute(chunk, 'row', [(8 * a + k, 8 * b + k) for a, b in pairs for...  12.6 us
    pallas_call x3, Pallas kernels, products(): pl.pallas_call(functools.partial(product_kernel, hops), out_shape=[jax.Sh...  12.4 us
    ppermute x1, starting transfers between devices, spread(): near = lax.ppermute(a_blocks, 'col', [(0, 3), (1, 4)])  9.26 us
    ppermute x1, starting transfers between devices, spread(): far = lax.ppermute(a_blocks, 'col', [(0, 9), (1, 10)])  5.25 us
  transfers between devices with their start and end apart: 24, of which 8 were waited for; matrix products, arithmetic and copies ran while one was open for 5% of the time, Pallas kernels for 6%

profile of v2, /device:TPU:80, one launch (start us, length us, event | category | flops | bytes accessed | tf_op | source)
XLA Modules:
  0.0 134.2 jit_solution(611362053224141011)
XLA Ops:
  0.0 9.3 %collective-permute-start.11 = (bf16[16,128,128]{2,1,0:T(8,128)(2,1)}, bf16[16,128,128]{2,1,0:T(8,128)(2,1)S(1)}, u32[]{:S(2)}, u32[]{:S(2)}) collective-permute-start(bf16[16,128,128]{2,1,0:T(8,128)(2,1)} %param.5), channel_id=1, source_target_pairs={{0,3},{1,4},{12,15},{13,16},{24,27},{25,28},{36,39},{37,40},{48,51... | collective-permute-start | bytes 1572872 | tf_op jit(solution)/shard_map/ppermute | solution.py:154
  9.3 5.3 %collective-permute-start.12 = (bf16[16,128,128]{2,1,0:T(8,128)(2,1)}, bf16[16,128,128]{2,1,0:T(8,128)(2,1)S(1)}, u32[]{:S(2)}, u32[]{:S(2)}) collective-permute-start(bf16[16,128,128]{2,1,0:T(8,128)(2,1)} %param.5), channel_id=1, source_target_pairs={{0,9},{1,10},{12,21},{13,22},{24,33},{25,34},{36,45},{37,46},{48,5... | collective-permute-start | bytes 1572872 | tf_op jit(solution)/shard_map/ppermute | solution.py:155
  25.0 12.6 %collective-permute-done.5 = bf16[4,128,128]{2,1,0:T(8,128)(2,1)S(1)} collective-permute-done((bf16[4,128,128]{2,1,0:T(8,128)(2,1)S(1)}, bf16[4,128,128]{2,1,0:T(8,128)(2,1)S(1)}, u32[]{:S(2)}, u32[]{:S(2)}) %collective-permute-start.5) | collective-permute-done | bytes 131104 | tf_op jit(solution)/shard_map/ppermute | solution.py:144
  37.6 1.9 %collective-permute-start.8 = (bf16[544,128]{1,0:T(8,128)(2,1)S(1)}, bf16[544,128]{1,0:T(8,128)(2,1)S(1)}, u32[]{:S(2)}, u32[]{:S(2)}) collective-permute-start(bf16[544,128]{1,0:T(8,128)(2,1)S(1)} %pad_maximum_fusion.1), channel_id=1, source_target_pairs={{0,4},{1,5},{2,6},{3,7},{4,8},{5,9},{6,10},{7,11},{8,0},{9,1},{10,... | collective-permute-start | bytes 417800 | tf_op jit(solution)/shard_map/ppermute | solution.py:128
  39.6 7.8 %collective-permute-start.7 = (bf16[544,128]{1,0:T(8,128)(2,1)S(1)}, bf16[544,128]{1,0:T(8,128)(2,1)S(1)}, u32[]{:S(2)}, u32[]{:S(2)}) collective-permute-start(bf16[544,128]{1,0:T(8,128)(2,1)S(1)} %pad_maximum_fusion.1), channel_id=1, source_target_pairs={{0,8},{1,9},{2,10},{3,11},{4,0},{5,1},{6,2},{7,3},{8,4},{9,5},{10,... | collective-permute-start | bytes 417800 | tf_op jit(solution)/shard_map/ppermute | solution.py:128
  48.9 6.0 %collective-permute-done.8 = bf16[544,128]{1,0:T(8,128)(2,1)S(1)} collective-permute-done((bf16[544,128]{1,0:T(8,128)(2,1)S(1)}, bf16[544,128]{1,0:T(8,128)(2,1)S(1)}, u32[]{:S(2)}, u32[]{:S(2)}) %collective-permute-start.8) | collective-permute-done | bytes 139296 | tf_op jit(solution)/shard_map/ppermute | solution.py:128
  55.1 2.9 %collective-permute-start.10 = (bf16[12,128,128]{2,1,0:T(8,128)(2,1)S(1)}, bf16[12,128,128]{2,1,0:T(8,128)(2,1)S(1)}, u32[]{:S(2)}, u32[]{:S(2)}) collective-permute-start(bf16[12,128,128]{2,1,0:T(8,128)(2,1)S(1)} %pad_maximum_fusion), channel_id=1, source_target_pairs={{0,24},{12,36},{24,48},{36,60},{48,72},{60,84},{72,0},{84,12},{96,... | collective-permute-start | bytes 1179656 | tf_op jit(solution)/shard_map/ppermute | solution.py:132
  58.0 4.1 %collective-permute-start.9 = (bf16[12,128,128]{2,1,0:T(8,128)(2,1)S(1)}, bf16[12,128,128]{2,1,0:T(8,128)(2,1)S(1)}, u32[]{:S(2)}, u32[]{:S(2)}) collective-permute-start(bf16[12,128,128]{2,1,0:T(8,128)(2,1)S(1)} %pad_maximum_fusion), channel_id=1, source_target_pairs={{0,72},{12,84},{24,0},{36,12},{48,24},{60,36},{72,48},{84,60},{96,... | collective-permute-start | bytes 1179656 | tf_op jit(solution)/shard_map/ppermute | solution.py:132
  63.3 5.9 %collective-permute-done.10 = bf16[12,128,128]{2,1,0:T(8,128)(2,1)S(1)} collective-permute-done((bf16[12,128,128]{2,1,0:T(8,128)(2,1)S(1)}, bf16[12,128,128]{2,1,0:T(8,128)(2,1)S(1)}, u32[]{:S(2)}, u32[]{:S(2)}) %collective-permute-start.10) | collective-permute-done | bytes 393248 | tf_op jit(solution)/shard_map/ppermute | solution.py:132
  69.2 2.3 %collective-permute-done.9 = bf16[12,128,128]{2,1,0:T(8,128)(2,1)S(1)} collective-permute-done((bf16[12,128,128]{2,1,0:T(8,128)(2,1)S(1)}, bf16[12,128,128]{2,1,0:T(8,128)(2,1)S(1)}, u32[]{:S(2)}, u32[]{:S(2)}) %collective-permute-start.9) | collective-permute-done | bytes 393248 | tf_op jit(solution)/shard_map/ppermute | solution.py:132
  71.4 3.2 %collective-permute-start.18 = (bf16[16,128,128]{2,1,0:T(8,128)(2,1)S(1)}, bf16[16,128,128]{2,1,0:T(8,128)(2,1)S(1)}, u32[]{:S(2)}, u32[]{:S(2)}) collective-permute-start(bf16[16,128,128]{2,1,0:T(8,128)(2,1)S(1)} %join.1.own), channel_id=1, source_target_pairs={{0,11},{1,0},{3,2},{4,3},{6,5},{7,6},{9,8},{10,9},{12,23},{13,12},... | collective-permute-start | bytes 1572872 | tf_op jit(solution)/shard_map/ppermute | solution.py:178
  74.6 1.9 %collective-permute-start.17 = (bf16[16,128,128]{2,1,0:T(8,128)(2,1)S(1)}, bf16[16,128,128]{2,1,0:T(8,128)(2,1)S(1)}, u32[]{:S(2)}, u32[]{:S(2)}) collective-permute-start(bf16[16,128,128]{2,1,0:T(8,128)(2,1)S(1)} %join.1.own), channel_id=1, source_target_pairs={{0,1},{1,2},{3,4},{4,5},{6,7},{7,8},{9,10},{10,11},{12,13},{13,14}... | collective-permute-start | bytes 1572872 | tf_op jit(solution)/shard_map/ppermute | solution.py:177
  76.6 4.4 %collective-permute-start.15 = (bf16[6,128,128]{2,1,0:T(8,128)(2,1)S(1)}, bf16[6,128,128]{2,1,0:T(8,128)(2,1)S(1)}, u32[]{:S(2)}, u32[]{:S(2)}) collective-permute-start(bf16[6,128,128]{2,1,0:T(8,128)(2,1)S(1)} %slice.110), channel_id=1, source_target_pairs={{0,72},{12,84},{24,0},{36,12},{48,24},{60,36},{72,48},{84,60},{96,... | collective-permute-start | bytes 589832 | tf_op jit(solution)/shard_map/ppermute | solution.py:132
  81.2 1.9 %collective-permute-start.16 = (bf16[6,128,128]{2,1,0:T(8,128)(2,1)S(1)}, bf16[6,128,128]{2,1,0:T(8,128)(2,1)S(1)}, u32[]{:S(2)}, u32[]{:S(2)}) collective-permute-start(bf16[6,128,128]{2,1,0:T(8,128)(2,1)S(1)} %slice.111), channel_id=1, source_target_pairs={{0,24},{12,36},{24,48},{36,60},{48,72},{60,84},{72,0},{84,12},{96,... | collective-permute-start | bytes 589832 | tf_op jit(solution)/shard_map/ppermute | solution.py:132
  84.2 5.8 %collective-permute-done.16 = bf16[6,128,128]{2,1,0:T(8,128)(2,1)S(1)} collective-permute-done((bf16[6,128,128]{2,1,0:T(8,128)(2,1)S(1)}, bf16[6,128,128]{2,1,0:T(8,128)(2,1)S(1)}, u32[]{:S(2)}, u32[]{:S(2)}) %collective-permute-start.16) | collective-permute-done | bytes 196640 | tf_op jit(solution)/shard_map/ppermute | solution.py:132
  90.1 1.9 %collective-permute-start.19 = (bf16[48,128,128]{2,1,0:T(8,128)(2,1)S(1)}, bf16[48,128,128]{2,1,0:T(8,128)(2,1)S(1)}, u32[]{:S(2)}, u32[]{:S(2)}) collective-permute-start(bf16[48,128,128]{2,1,0:T(8,128)(2,1)S(1)} %constant_dynamic-update-slice_fusion.right_own), channel_id=1, source_target_pairs={{0,12},{12,0},{24,36},{36,24},{48,60},{60,48},{72,84},{84,72},{96,... | collective-permute-start | bytes 4718600 | tf_op jit(solution)/shard_map/ppermute | solution.py:182
  92.8 2.6 %collective-permute-done.19.right_other = bf16[48,128,128]{2,1,0:T(8,128)(2,1)S(1)} collective-permute-done((bf16[48,128,128]{2,1,0:T(8,128)(2,1)S(1)}, bf16[48,128,128]{2,1,0:T(8,128)(2,1)S(1)}, u32[]{:S(2)}, u32[]{:S(2)}) %collective-permute-start.19) | collective-permute-done | bytes 1572896 | tf_op jit(solution)/shard_map/ppermute | solution.py:182
  95.4 4.5 %products.4 = (bf16[12,128,128]{2,1,0:T(8,128)(2,1)S(1)}, bf16[12,128,128]{2,1,0:T(8,128)(2,1)S(1)}) custom-call(s32[75,128]{1,0:T(8,128)S(1)} %fusion.1.table, bf16[16,128,128]{2,1,0:T(8,128)(2,1)S(1)} %join.1.own, bf16[16,128,128]{2,1,0:T(8,128)(2,1)S(1)} %collective-permute-done.17.from_low, bf16[16,128,128]{2,1,0:T(8,128)(2,1)S(1)} %collective-permute-done.18.from_high, ...), custom_call_target="tpu_custom_call" | custom-call | flops 1610612736 | bytes 4194304 | tf_op jit(solution)/shard_map/products/pallas_call | solution.py:237
  99.8 6.0 %collective-permute-start.22 = (bf16[12,128,128]{2,1,0:T(8,128)(2,1)S(1)}, bf16[12,128,128]{2,1,0:T(8,128)(2,1)S(1)}, u32[]{:S(2)}, u32[]{:S(2)}) collective-permute-start(bf16[12,128,128]{2,1,0:T(8,128)(2,1)S(1)} %get-tuple-element.23), channel_id=1, source_target_pairs={{0,11},{1,0},{2,1},{3,2},{4,3},{5,4},{6,5},{7,6},{8,7},{9,8},{10,9... | collective-permute-start | bytes 1179656 | tf_op jit(solution)/shard_map/ppermute | solution.py:128
  105.8 1.9 %collective-permute-start.23 = (bf16[12,128,128]{2,1,0:T(8,128)(2,1)S(1)}, bf16[12,128,128]{2,1,0:T(8,128)(2,1)S(1)}, u32[]{:S(2)}, u32[]{:S(2)}) collective-permute-start(bf16[12,128,128]{2,1,0:T(8,128)(2,1)S(1)} %get-tuple-element.24), channel_id=1, source_target_pairs={{0,1},{1,2},{2,3},{3,4},{4,5},{5,6},{6,7},{7,8},{8,9},{9,10},{10,1... | collective-permute-start | bytes 1179656 | tf_op jit(solution)/shard_map/ppermute | solution.py:128
  107.8 4.6 %products.3 = (bf16[4,128,128]{2,1,0:T(8,128)(2,1)S(1)}, bf16[8,128,128]{2,1,0:T(8,128)(2,1)S(1)}) custom-call(s32[75,128]{1,0:T(8,128)S(1)} %fusion.1.table, bf16[16,128,128]{2,1,0:T(8,128)(2,1)S(1)} %join.1.own, bf16[16,128,128]{2,1,0:T(8,128)(2,1)S(1)} %collective-permute-done.17.from_low, bf16[16,128,128]{2,1,0:T(8,128)(2,1)S(1)} %collective-permute-done.18.from_high, ...), custom_call_target="tpu_custom_call" | custom-call | flops 805306368 | bytes 4194304 | tf_op jit(solution)/shard_map/products/pallas_call | solution.py:237
  112.4 7.2 %collective-permute-start.21 = (bf16[8,128,128]{2,1,0:T(8,128)(2,1)S(1)}, bf16[8,128,128]{2,1,0:T(8,128)(2,1)S(1)}, u32[]{:S(2)}, u32[]{:S(2)}) collective-permute-start(bf16[8,128,128]{2,1,0:T(8,128)(2,1)S(1)} %get-tuple-element.22), channel_id=1, source_target_pairs={{0,2},{1,3},{2,4},{3,5},{4,6},{5,7},{6,8},{7,9},{8,10},{9,11},{10,... | collective-permute-start | bytes 786440 | tf_op jit(solution)/shard_map/ppermute | solution.py:128
  121.5 3.4 %products.5.refs_4_ = bf16[12,128,128]{2,1,0:T(8,128)(2,1)S(1)} custom-call(s32[75,128]{1,0:T(8,128)S(1)} %fusion.1.table, bf16[16,128,128]{2,1,0:T(8,128)(2,1)S(1)} %join.1.own, bf16[16,128,128]{2,1,0:T(8,128)(2,1)S(1)} %collective-permute-done.17.from_low, bf16[16,128,128]{2,1,0:T(8,128)(2,1)S(1)} %collective-permute-done.18.from_high, ...), custom_call_target="tpu_custom_call" | custom-call | flops 805306368 | bytes 4194304 | tf_op jit(solution)/shard_map/products/pallas_call | solution.py:237
  124.9 8.0 %collective-permute-done.20.refs_0_ = bf16[4,128,128]{2,1,0:T(8,128)(2,1)S(1)} collective-permute-done((bf16[4,128,128]{2,1,0:T(8,128)(2,1)S(1)}, bf16[4,128,128]{2,1,0:T(8,128)(2,1)S(1)}, u32[]{:S(2)}, u32[]{:S(2)}) %collective-permute-start.20) | collective-permute-done | bytes 131104 | tf_op jit(solution)/shard_map/ppermute | solution.py:128
  (93 shorter events, 18.1 us)
Async XLA Ops:
  0.0 47.4 %collective-permute-start.11 = (bf16[16,128,128]{2,1,0:T(8,128)(2,1)}, bf16[16,128,128]{2,1,0:T(8,128)(2,1)S(1)}, u32[]{:S(2)}, u32[]{:S(2)}) collective-permute-start(bf16[16,128,128]{2,1,0:T(8,128)(2,1)} %param.5), channel_id=1, source_target_pairs={{0,3},{1,4},{12,15},{13,16},{24,27},{25,28},{36,39},{37,40},{48,51... | collective-permute-start | bytes 1572872 | tf_op jit(solution)/shard_map/ppermute | solution.py:154
  9.3 38.1 %collective-permute-start.12 = (bf16[16,128,128]{2,1,0:T(8,128)(2,1)}, bf16[16,128,128]{2,1,0:T(8,128)(2,1)S(1)}, u32[]{:S(2)}, u32[]{:S(2)}) collective-permute-start(bf16[16,128,128]{2,1,0:T(8,128)(2,1)} %param.5), channel_id=1, source_target_pairs={{0,9},{1,10},{12,21},{13,22},{24,33},{25,34},{36,45},{37,46},{48,5... | collective-permute-start | bytes 1572872 | tf_op jit(solution)/shard_map/ppermute | solution.py:155
  15.6 4.5 %collective-permute-start.2 = (bf16[4,128,128]{2,1,0:T(8,128)(2,1)S(1)}, bf16[4,128,128]{2,1,0:T(8,128)(2,1)S(1)}, u32[]{:S(2)}, u32[]{:S(2)}) collective-permute-start(bf16[4,128,128]{2,1,0:T(8,128)(2,1)S(1)} %get-tuple-element.37), channel_id=1, source_target_pairs={{0,24},{12,36},{1,25},{13,37},{2,26},{14,38},{3,27},{15,39},{4,28}... | collective-permute-start | bytes 393224 | tf_op jit(solution)/shard_map/ppermute | solution.py:138
  16.3 3.8 %collective-permute-start.1 = (bf16[4,128,128]{2,1,0:T(8,128)(2,1)S(1)}, bf16[4,128,128]{2,1,0:T(8,128)(2,1)S(1)}, u32[]{:S(2)}, u32[]{:S(2)}) collective-permute-start(bf16[4,128,128]{2,1,0:T(8,128)(2,1)S(1)} %get-tuple-element.38), channel_id=1, source_target_pairs={{0,48},{12,60},{1,49},{13,61},{2,50},{14,62},{3,51},{15,63},{4,52}... | collective-permute-start | bytes 393224 | tf_op jit(solution)/shard_map/ppermute | solution.py:138
  16.9 3.2 %collective-permute-start = (bf16[4,128,128]{2,1,0:T(8,128)(2,1)S(1)}, bf16[4,128,128]{2,1,0:T(8,128)(2,1)S(1)}, u32[]{:S(2)}, u32[]{:S(2)}) collective-permute-start(bf16[4,128,128]{2,1,0:T(8,128)(2,1)S(1)} %get-tuple-element.39), channel_id=1, source_target_pairs={{0,72},{12,84},{1,73},{13,85},{2,74},{14,86},{3,75},{15,87},{4,76}... | collective-permute-start | bytes 393224 | tf_op jit(solution)/shard_map/ppermute | solution.py:138
  21.1 1.6 %collective-permute-start.4 = (bf16[4,128,128]{2,1,0:T(8,128)(2,1)S(1)}, bf16[4,128,128]{2,1,0:T(8,128)(2,1)S(1)}, u32[]{:S(2)}, u32[]{:S(2)}) collective-permute-start(bf16[4,128,128]{2,1,0:T(8,128)(2,1)S(1)} %select_select_fusion.3), channel_id=1, source_target_pairs={{0,288},{12,300},{24,312},{36,324},{48,336},{60,348},{72,360},{84,... | collective-permute-start | bytes 393224 | tf_op jit(solution)/shard_map/ppermute | solution.py:144
  21.7 0.9 collective-permute-start.3
  22.7 2.3 %collective-permute-start.6 = (bf16[4,128,128]{2,1,0:T(8,128)(2,1)S(1)}, bf16[4,128,128]{2,1,0:T(8,128)(2,1)S(1)}, u32[]{:S(2)}, u32[]{:S(2)}) collective-permute-start(bf16[4,128,128]{2,1,0:T(8,128)(2,1)S(1)} %select_select_fusion.2), channel_id=1, source_target_pairs={{0,96},{12,108},{24,120},{36,132},{48,144},{60,156},{72,168},{84,1... | collective-permute-start | bytes 393224 | tf_op jit(solution)/shard_map/ppermute | solution.py:144
  23.4 14.2 %collective-permute-start.5 = (bf16[4,128,128]{2,1,0:T(8,128)(2,1)S(1)}, bf16[4,128,128]{2,1,0:T(8,128)(2,1)S(1)}, u32[]{:S(2)}, u32[]{:S(2)}) collective-permute-start(bf16[4,128,128]{2,1,0:T(8,128)(2,1)S(1)} %select_select_fusion.2), channel_id=1, source_target_pairs={{0,672},{12,684},{24,696},{36,708},{48,720},{60,732},{72,744},{84,... | collective-permute-start | bytes 393224 | tf_op jit(solution)/shard_map/ppermute | solution.py:144
  37.6 17.3 %collective-permute-start.8 = (bf16[544,128]{1,0:T(8,128)(2,1)S(1)}, bf16[544,128]{1,0:T(8,128)(2,1)S(1)}, u32[]{:S(2)}, u32[]{:S(2)}) collective-permute-start(bf16[544,128]{1,0:T(8,128)(2,1)S(1)} %pad_maximum_fusion.1), channel_id=1, source_target_pairs={{0,4},{1,5},{2,6},{3,7},{4,8},{5,9},{6,10},{7,11},{8,0},{9,1},{10,... | collective-permute-start | bytes 417800 | tf_op jit(solution)/shard_map/ppermute | solution.py:128
  39.6 15.4 %collective-permute-start.7 = (bf16[544,128]{1,0:T(8,128)(2,1)S(1)}, bf16[544,128]{1,0:T(8,128)(2,1)S(1)}, u32[]{:S(2)}, u32[]{:S(2)}) collective-permute-start(bf16[544,128]{1,0:T(8,128)(2,1)S(1)} %pad_maximum_fusion.1), channel_id=1, source_target_pairs={{0,8},{1,9},{2,10},{3,11},{4,0},{5,1},{6,2},{7,3},{8,4},{9,5},{10,... | collective-permute-start | bytes 417800 | tf_op jit(solution)/shard_map/ppermute | solution.py:128
  47.5 15.7 %collective-permute-start.14 = (bf16[8,128,128]{2,1,0:T(8,128)(2,1)S(1)}, bf16[8,128,128]{2,1,0:T(8,128)(2,1)S(1)}, u32[]{:S(2)}, u32[]{:S(2)}) collective-permute-start(bf16[8,128,128]{2,1,0:T(8,128)(2,1)S(1)} %get-tuple-element.35), channel_id=1, source_target_pairs={{9,6},{10,7},{21,18},{22,19},{33,30},{34,31},{45,42},{46,43},{57,5... | collective-permute-start | bytes 786440 | tf_op jit(solution)/shard_map/ppermute | solution.py:163
  48.2 15.0 %collective-permute-start.13 = (bf16[8,128,128]{2,1,0:T(8,128)(2,1)S(1)}, bf16[8,128,128]{2,1,0:T(8,128)(2,1)S(1)}, u32[]{:S(2)}, u32[]{:S(2)}) collective-permute-start(bf16[8,128,128]{2,1,0:T(8,128)(2,1)S(1)} %get-tuple-element.36), channel_id=1, source_target_pairs={{3,6},{4,7},{15,18},{16,19},{27,30},{28,31},{39,42},{40,43},{51,54... | collective-permute-start | bytes 786440 | tf_op jit(solution)/shard_map/ppermute | solution.py:162
  55.1 14.1 %collective-permute-start.10 = (bf16[12,128,128]{2,1,0:T(8,128)(2,1)S(1)}, bf16[12,128,128]{2,1,0:T(8,128)(2,1)S(1)}, u32[]{:S(2)}, u32[]{:S(2)}) collective-permute-start(bf16[12,128,128]{2,1,0:T(8,128)(2,1)S(1)} %pad_maximum_fusion), channel_id=1, source_target_pairs={{0,24},{12,36},{24,48},{36,60},{48,72},{60,84},{72,0},{84,12},{96,... | collective-permute-start | bytes 1179656 | tf_op jit(solution)/shard_map/ppermute | solution.py:132
  58.0 13.4 %collective-permute-start.9 = (bf16[12,128,128]{2,1,0:T(8,128)(2,1)S(1)}, bf16[12,128,128]{2,1,0:T(8,128)(2,1)S(1)}, u32[]{:S(2)}, u32[]{:S(2)}) collective-permute-start(bf16[12,128,128]{2,1,0:T(8,128)(2,1)S(1)} %pad_maximum_fusion), channel_id=1, source_target_pairs={{0,72},{12,84},{24,0},{36,12},{48,24},{60,36},{72,48},{84,60},{96,... | collective-permute-start | bytes 1179656 | tf_op jit(solution)/shard_map/ppermute | solution.py:132
  71.4 18.6 %collective-permute-start.18 = (bf16[16,128,128]{2,1,0:T(8,128)(2,1)S(1)}, bf16[16,128,128]{2,1,0:T(8,128)(2,1)S(1)}, u32[]{:S(2)}, u32[]{:S(2)}) collective-permute-start(bf16[16,128,128]{2,1,0:T(8,128)(2,1)S(1)} %join.1.own), channel_id=1, source_target_pairs={{0,11},{1,0},{3,2},{4,3},{6,5},{7,6},{9,8},{10,9},{12,23},{13,12},... | collective-permute-start | bytes 1572872 | tf_op jit(solution)/shard_map/ppermute | solution.py:178
  74.6 15.4 %collective-permute-start.17 = (bf16[16,128,128]{2,1,0:T(8,128)(2,1)S(1)}, bf16[16,128,128]{2,1,0:T(8,128)(2,1)S(1)}, u32[]{:S(2)}, u32[]{:S(2)}) collective-permute-start(bf16[16,128,128]{2,1,0:T(8,128)(2,1)S(1)} %join.1.own), channel_id=1, source_target_pairs={{0,1},{1,2},{3,4},{4,5},{6,7},{7,8},{9,10},{10,11},{12,13},{13,14}... | collective-permute-start | bytes 1572872 | tf_op jit(solution)/shard_map/ppermute | solution.py:177
  76.6 7.6 %collective-permute-start.15 = (bf16[6,128,128]{2,1,0:T(8,128)(2,1)S(1)}, bf16[6,128,128]{2,1,0:T(8,128)(2,1)S(1)}, u32[]{:S(2)}, u32[]{:S(2)}) collective-permute-start(bf16[6,128,128]{2,1,0:T(8,128)(2,1)S(1)} %slice.110), channel_id=1, source_target_pairs={{0,72},{12,84},{24,0},{36,12},{48,24},{60,36},{72,48},{84,60},{96,... | collective-permute-start | bytes 589832 | tf_op jit(solution)/shard_map/ppermute | solution.py:132
  81.2 8.8 %collective-permute-start.16 = (bf16[6,128,128]{2,1,0:T(8,128)(2,1)S(1)}, bf16[6,128,128]{2,1,0:T(8,128)(2,1)S(1)}, u32[]{:S(2)}, u32[]{:S(2)}) collective-permute-start(bf16[6,128,128]{2,1,0:T(8,128)(2,1)S(1)} %slice.111), channel_id=1, source_target_pairs={{0,24},{12,36},{24,48},{36,60},{48,72},{60,84},{72,0},{84,12},{96,... | collective-permute-start | bytes 589832 | tf_op jit(solution)/shard_map/ppermute | solution.py:132
  90.1 5.3 %collective-permute-start.19 = (bf16[48,128,128]{2,1,0:T(8,128)(2,1)S(1)}, bf16[48,128,128]{2,1,0:T(8,128)(2,1)S(1)}, u32[]{:S(2)}, u32[]{:S(2)}) collective-permute-start(bf16[48,128,128]{2,1,0:T(8,128)(2,1)S(1)} %constant_dynamic-update-slice_fusion.right_own), channel_id=1, source_target_pairs={{0,12},{12,0},{24,36},{36,24},{48,60},{60,48},{72,84},{84,72},{96,... | collective-permute-start | bytes 4718600 | tf_op jit(solution)/shard_map/ppermute | solution.py:182
  99.8 33.1 %collective-permute-start.22 = (bf16[12,128,128]{2,1,0:T(8,128)(2,1)S(1)}, bf16[12,128,128]{2,1,0:T(8,128)(2,1)S(1)}, u32[]{:S(2)}, u32[]{:S(2)}) collective-permute-start(bf16[12,128,128]{2,1,0:T(8,128)(2,1)S(1)} %get-tuple-element.23), channel_id=1, source_target_pairs={{0,11},{1,0},{2,1},{3,2},{4,3},{5,4},{6,5},{7,6},{8,7},{9,8},{10,9... | collective-permute-start | bytes 1179656 | tf_op jit(solution)/shard_map/ppermute | solution.py:128
  105.8 27.1 %collective-permute-start.23 = (bf16[12,128,128]{2,1,0:T(8,128)(2,1)S(1)}, bf16[12,128,128]{2,1,0:T(8,128)(2,1)S(1)}, u32[]{:S(2)}, u32[]{:S(2)}) collective-permute-start(bf16[12,128,128]{2,1,0:T(8,128)(2,1)S(1)} %get-tuple-element.24), channel_id=1, source_target_pairs={{0,1},{1,2},{2,3},{3,4},{4,5},{5,6},{6,7},{7,8},{8,9},{9,10},{10,1... | collective-permute-start | bytes 1179656 | tf_op jit(solution)/shard_map/ppermute | solution.py:128
  112.4 20.5 %collective-permute-start.21 = (bf16[8,128,128]{2,1,0:T(8,128)(2,1)S(1)}, bf16[8,128,128]{2,1,0:T(8,128)(2,1)S(1)}, u32[]{:S(2)}, u32[]{:S(2)}) collective-permute-start(bf16[8,128,128]{2,1,0:T(8,128)(2,1)S(1)} %get-tuple-element.22), channel_id=1, source_target_pairs={{0,2},{1,3},{2,4},{3,5},{4,6},{5,7},{6,8},{7,9},{8,10},{9,11},{10,... | collective-permute-start | bytes 786440 | tf_op jit(solution)/shard_map/ppermute | solution.py:128
  119.6 13.3 %collective-permute-start.20 = (bf16[4,128,128]{2,1,0:T(8,128)(2,1)S(1)}, bf16[4,128,128]{2,1,0:T(8,128)(2,1)S(1)}, u32[]{:S(2)}, u32[]{:S(2)}) collective-permute-start(bf16[4,128,128]{2,1,0:T(8,128)(2,1)S(1)} %get-tuple-element.21), channel_id=1, source_target_pairs={{0,10},{1,11},{2,0},{3,1},{4,2},{5,3},{6,4},{7,5},{8,6},{9,7},{10,... | collective-permute-start | bytes 393224 | tf_op jit(solution)/shard_map/ppermute | solution.py:128
  (4 other events, 112.0 us)

commit v3 on v2

--- a/solution.py
+++ b/solution.py
@@ -172,7 +172,6 @@
     )(jnp.full((1,), third, jnp.int32), own, low, high)
 
     after, behind = x_shift(held, 1), x_shift(held, 3)
-    after, behind, own = lax.optimization_barrier((after, behind, own))
     half = HELD * QUARTER // 2
     from_low = lax.ppermute(own, "col", [(z, (z + 1) % 12) for z in range(12) if z % 3 < 2])
     from_high = lax.ppermute(own, "col", [(z, (z - 1) % 12) for z in range(12) if z % 3 < 2])
@@ -245,9 +244,8 @@
             name="products",
         )(table, own, from_low, from_high, right_own, right_other)
 
-    made = []
-    for distance in sorted({abs(h) for h in ROUTES}, reverse=True):
-        made += products(tuple(h for h in ROUTES if abs(h) == distance))
+    away = tuple(h for h in ROUTES if h != 0)
+    made = products(away) + products((0,))
     arrived = [part if hop == 0 else shift(part, "col", N_COL, hop) for part, hop in zip(made, ROUTES)]
     return pl.pallas_call(
         place_kernel,

time: 135 us -> 130 us (0.963)
  the two profiles are of different devices: /device:TPU:80 before, /device:TPU:112 now
where the time goes in v3:
time: 130 us; the launch traced here: 128 us
  starting transfers between devices  69.4 us (53%)
  waiting for transfers between devices  39.5 us (30%)
  Pallas kernels  11.5 us (9%)
  local copies, waits for them, and re-layouts  3.69 us (3%)
  other arithmetic  3.51 us (3%)
    ppermute x6, starting transfers between devices, shift(): lax.ppermute(value, axis, [(i, (i + hop) % size) for i in range(size)])  26.7 us
    ppermute x6, waiting for transfers between devices, shift(): lax.ppermute(value, axis, [(i, (i + hop) % size) for i in range(size)])  15.9 us
    ppermute x4, starting transfers between devices, x_shift(): lax.ppermute(value, 'row', [(8 * y + 2 * x + q, 8 * y + 2 * ((x - hop) %...  13.7 us
    ppermute x4, waiting for transfers between devices, spread_chunk(): lax.ppermute(chunk, 'row', [(8 * a + k, 8 * b + k) for a, b in pairs for...  12.3 us
    pallas_call x2, Pallas kernels, products(): pl.pallas_call(functools.partial(product_kernel, hops), out_shape=[jax.Sh...  10.1 us
    ppermute x1, starting transfers between devices, spread(): near = lax.ppermute(a_blocks, 'col', [(0, 3), (1, 4)])  9.26 us
    ppermute x4, waiting for transfers between devices, x_shift(): lax.ppermute(value, 'row', [(8 * y + 2 * x + q, 8 * y + 2 * ((x - hop) %...  8.73 us
    ppermute x1, starting transfers between devices, spread(): far = lax.ppermute(a_blocks, 'col', [(0, 9), (1, 10)])  5.25 us
  transfers between devices with their start and end apart: 24, of which 8 were waited for; matrix products, arithmetic and copies ran while one was open for 6% of the time, Pallas kernels for 3%

profile of v3, /device:TPU:112, one launch (start us, length us, event | category | flops | bytes accessed | tf_op | source)
XLA Modules:
  0.0 128.3 jit_solution(7873605805999405309)
XLA Ops:
  0.0 9.3 %collective-permute-start.9 = (bf16[16,128,128]{2,1,0:T(8,128)(2,1)}, bf16[16,128,128]{2,1,0:T(8,128)(2,1)S(1)}, u32[]{:S(2)}, u32[]{:S(2)}) collective-permute-start(bf16[16,128,128]{2,1,0:T(8,128)(2,1)} %param.5), channel_id=1, source_target_pairs={{0,3},{1,4},{12,15},{13,16},{24,27},{25,28},{36,39},{37,40},{48,51... | collective-permute-start | bytes 1572872 | tf_op jit(solution)/shard_map/ppermute | solution.py:154
  9.3 5.3 %collective-permute-start.10 = (bf16[16,128,128]{2,1,0:T(8,128)(2,1)}, bf16[16,128,128]{2,1,0:T(8,128)(2,1)S(1)}, u32[]{:S(2)}, u32[]{:S(2)}) collective-permute-start(bf16[16,128,128]{2,1,0:T(8,128)(2,1)} %param.5), channel_id=1, source_target_pairs={{0,9},{1,10},{12,21},{13,22},{24,33},{25,34},{36,45},{37,46},{48,5... | collective-permute-start | bytes 1572872 | tf_op jit(solution)/shard_map/ppermute | solution.py:155
  25.0 12.3 %collective-permute-done.6 = bf16[4,128,128]{2,1,0:T(8,128)(2,1)S(1)} collective-permute-done((bf16[4,128,128]{2,1,0:T(8,128)(2,1)S(1)}, bf16[4,128,128]{2,1,0:T(8,128)(2,1)S(1)}, u32[]{:S(2)}, u32[]{:S(2)}) %collective-permute-start.6) | collective-permute-done | bytes 131104 | tf_op jit(solution)/shard_map/ppermute | solution.py:144
  37.3 1.9 %collective-permute-start.8 = (bf16[544,128]{1,0:T(8,128)(2,1)S(1)}, bf16[544,128]{1,0:T(8,128)(2,1)S(1)}, u32[]{:S(2)}, u32[]{:S(2)}) collective-permute-start(bf16[544,128]{1,0:T(8,128)(2,1)S(1)} %pad_maximum_fusion.1), channel_id=1, source_target_pairs={{0,4},{1,5},{2,6},{3,7},{4,8},{5,9},{6,10},{7,11},{8,0},{9,1},{10,... | collective-permute-start | bytes 417800 | tf_op jit(solution)/shard_map/ppermute | solution.py:128
  39.2 7.8 %collective-permute-start.7 = (bf16[544,128]{1,0:T(8,128)(2,1)S(1)}, bf16[544,128]{1,0:T(8,128)(2,1)S(1)}, u32[]{:S(2)}, u32[]{:S(2)}) collective-permute-start(bf16[544,128]{1,0:T(8,128)(2,1)S(1)} %pad_maximum_fusion.1), channel_id=1, source_target_pairs={{0,8},{1,9},{2,10},{3,11},{4,0},{5,1},{6,2},{7,3},{8,4},{9,5},{10,... | collective-permute-start | bytes 417800 | tf_op jit(solution)/shard_map/ppermute | solution.py:128
  48.6 6.2 %collective-permute-done.8 = bf16[544,128]{1,0:T(8,128)(2,1)S(1)} collective-permute-done((bf16[544,128]{1,0:T(8,128)(2,1)S(1)}, bf16[544,128]{1,0:T(8,128)(2,1)S(1)}, u32[]{:S(2)}, u32[]{:S(2)}) %collective-permute-start.8) | collective-permute-done | bytes 139296 | tf_op jit(solution)/shard_map/ppermute | solution.py:128
  54.9 3.5 %collective-permute-start.15 = (bf16[12,128,128]{2,1,0:T(8,128)(2,1)S(1)}, bf16[12,128,128]{2,1,0:T(8,128)(2,1)S(1)}, u32[]{:S(2)}, u32[]{:S(2)}) collective-permute-start(bf16[12,128,128]{2,1,0:T(8,128)(2,1)S(1)} %pad_maximum_fusion), channel_id=1, source_target_pairs={{0,24},{12,36},{24,48},{36,60},{48,72},{60,84},{72,0},{84,12},{96,... | collective-permute-start | bytes 1179656 | tf_op jit(solution)/shard_map/ppermute | solution.py:132
  58.4 3.6 %collective-permute-start.13 = (bf16[12,128,128]{2,1,0:T(8,128)(2,1)S(1)}, bf16[12,128,128]{2,1,0:T(8,128)(2,1)S(1)}, u32[]{:S(2)}, u32[]{:S(2)}) collective-permute-start(bf16[12,128,128]{2,1,0:T(8,128)(2,1)S(1)} %pad_maximum_fusion), channel_id=1, source_target_pairs={{0,72},{12,84},{24,0},{36,12},{48,24},{60,36},{72,48},{84,60},{96,... | collective-permute-start | bytes 1179656 | tf_op jit(solution)/shard_map/ppermute | solution.py:132
  63.1 4.0 %collective-permute-start.18 = (bf16[16,128,128]{2,1,0:T(8,128)(2,1)S(1)}, bf16[16,128,128]{2,1,0:T(8,128)(2,1)S(1)}, u32[]{:S(2)}, u32[]{:S(2)}) collective-permute-start(bf16[16,128,128]{2,1,0:T(8,128)(2,1)S(1)} %join.1.own), channel_id=1, source_target_pairs={{0,11},{1,0},{3,2},{4,3},{6,5},{7,6},{9,8},{10,9},{12,23},{13,12},... | collective-permute-start | bytes 1572872 | tf_op jit(solution)/shard_map/ppermute | solution.py:177
  67.1 1.9 %collective-permute-start.17 = (bf16[16,128,128]{2,1,0:T(8,128)(2,1)S(1)}, bf16[16,128,128]{2,1,0:T(8,128)(2,1)S(1)}, u32[]{:S(2)}, u32[]{:S(2)}) collective-permute-start(bf16[16,128,128]{2,1,0:T(8,128)(2,1)S(1)} %join.1.own), channel_id=1, source_target_pairs={{0,1},{1,2},{3,4},{4,5},{6,7},{7,8},{9,10},{10,11},{12,13},{13,14}... | collective-permute-start | bytes 1572872 | tf_op jit(solution)/shard_map/ppermute | solution.py:176
  69.0 2.0 %collective-permute-done.13 = bf16[12,128,128]{2,1,0:T(8,128)(2,1)S(1)} collective-permute-done((bf16[12,128,128]{2,1,0:T(8,128)(2,1)S(1)}, bf16[12,128,128]{2,1,0:T(8,128)(2,1)S(1)}, u32[]{:S(2)}, u32[]{:S(2)}) %collective-permute-start.13) | collective-permute-done | bytes 393248 | tf_op jit(solution)/shard_map/ppermute | solution.py:132
  71.0 4.8 %collective-permute-start.14 = (bf16[6,128,128]{2,1,0:T(8,128)(2,1)S(1)}, bf16[6,128,128]{2,1,0:T(8,128)(2,1)S(1)}, u32[]{:S(2)}, u32[]{:S(2)}) collective-permute-start(bf16[6,128,128]{2,1,0:T(8,128)(2,1)S(1)} %slice.131), channel_id=1, source_target_pairs={{0,72},{12,84},{24,0},{36,12},{48,24},{60,36},{72,48},{84,60},{96,... | collective-permute-start | bytes 589832 | tf_op jit(solution)/shard_map/ppermute | solution.py:132
  76.0 1.9 %collective-permute-start.16 = (bf16[6,128,128]{2,1,0:T(8,128)(2,1)S(1)}, bf16[6,128,128]{2,1,0:T(8,128)(2,1)S(1)}, u32[]{:S(2)}, u32[]{:S(2)}) collective-permute-start(bf16[6,128,128]{2,1,0:T(8,128)(2,1)S(1)} %slice.132), channel_id=1, source_target_pairs={{0,24},{12,36},{24,48},{36,60},{48,72},{60,84},{72,0},{84,12},{96,... | collective-permute-start | bytes 589832 | tf_op jit(solution)/shard_map/ppermute | solution.py:132
  79.0 5.8 %collective-permute-done.16 = bf16[6,128,128]{2,1,0:T(8,128)(2,1)S(1)} collective-permute-done((bf16[6,128,128]{2,1,0:T(8,128)(2,1)S(1)}, bf16[6,128,128]{2,1,0:T(8,128)(2,1)S(1)}, u32[]{:S(2)}, u32[]{:S(2)}) %collective-permute-start.16) | collective-permute-done | bytes 196640 | tf_op jit(solution)/shard_map/ppermute | solution.py:132
  84.9 1.9 %collective-permute-start.19 = (bf16[48,128,128]{2,1,0:T(8,128)(2,1)S(1)}, bf16[48,128,128]{2,1,0:T(8,128)(2,1)S(1)}, u32[]{:S(2)}, u32[]{:S(2)}) collective-permute-start(bf16[48,128,128]{2,1,0:T(8,128)(2,1)S(1)} %constant_dynamic-update-slice_fusion.right_own), channel_id=1, source_target_pairs={{0,12},{12,0},{24,36},{36,24},{48,60},{60,48},{72,84},{84,72},{96,... | collective-permute-start | bytes 4718600 | tf_op jit(solution)/shard_map/ppermute | solution.py:181
  87.6 2.6 %collective-permute-done.19.right_other = bf16[48,128,128]{2,1,0:T(8,128)(2,1)S(1)} collective-permute-done((bf16[48,128,128]{2,1,0:T(8,128)(2,1)S(1)}, bf16[48,128,128]{2,1,0:T(8,128)(2,1)S(1)}, u32[]{:S(2)}, u32[]{:S(2)}) %collective-permute-start.19) | collective-permute-done | bytes 1572896 | tf_op jit(solution)/shard_map/ppermute | solution.py:181
  90.2 6.8 %products.2 = (bf16[4,128,128]{2,1,0:T(8,128)(2,1)S(1)}, bf16[8,128,128]{2,1,0:T(8,128)(2,1)S(1)}, bf16[12,128,128]{2,1,0:T(8,128)(2,1)S(1)}, bf16[12,128,128]{2,1,0:T(8,128)(2,1)S(1)}) custom-call(s32[75,128]{1,0:T(8,128)S(1)} %fusion.1.table, bf16[16,128,128]{2,1,0:T(8,128)(2,1)S(1)} %join.1.own, ...), custom_call_target="tpu_custom_call" | custom-call | flops 2415919104 | bytes 4194304 | tf_op jit(solution)/shard_map/products/pallas_call | solution.py:236
  97.0 5.1 %collective-permute-start.22 = (bf16[12,128,128]{2,1,0:T(8,128)(2,1)S(1)}, bf16[12,128,128]{2,1,0:T(8,128)(2,1)S(1)}, u32[]{:S(2)}, u32[]{:S(2)}) collective-permute-start(bf16[12,128,128]{2,1,0:T(8,128)(2,1)S(1)} %get-tuple-element.17), channel_id=1, source_target_pairs={{0,11},{1,0},{2,1},{3,2},{4,3},{5,4},{6,5},{7,6},{8,7},{9,8},{10,9... | collective-permute-start | bytes 1179656 | tf_op jit(solution)/shard_map/ppermute | solution.py:128
  102.1 1.9 %collective-permute-start.23 = (bf16[12,128,128]{2,1,0:T(8,128)(2,1)S(1)}, bf16[12,128,128]{2,1,0:T(8,128)(2,1)S(1)}, u32[]{:S(2)}, u32[]{:S(2)}) collective-permute-start(bf16[12,128,128]{2,1,0:T(8,128)(2,1)S(1)} %get-tuple-element.18), channel_id=1, source_target_pairs={{0,1},{1,2},{2,3},{3,4},{4,5},{5,6},{6,7},{7,8},{8,9},{9,10},{10,1... | collective-permute-start | bytes 1179656 | tf_op jit(solution)/shard_map/ppermute | solution.py:128
  104.0 8.0 %collective-permute-start.21 = (bf16[8,128,128]{2,1,0:T(8,128)(2,1)S(1)}, bf16[8,128,128]{2,1,0:T(8,128)(2,1)S(1)}, u32[]{:S(2)}, u32[]{:S(2)}) collective-permute-start(bf16[8,128,128]{2,1,0:T(8,128)(2,1)S(1)} %get-tuple-element.16), channel_id=1, source_target_pairs={{0,2},{1,3},{2,4},{3,5},{4,6},{5,7},{6,8},{7,9},{8,10},{9,11},{10,... | collective-permute-start | bytes 786440 | tf_op jit(solution)/shard_map/ppermute | solution.py:128
  112.0 1.9 %collective-permute-start.20 = (bf16[4,128,128]{2,1,0:T(8,128)(2,1)S(1)}, bf16[4,128,128]{2,1,0:T(8,128)(2,1)S(1)}, u32[]{:S(2)}, u32[]{:S(2)}) collective-permute-start(bf16[4,128,128]{2,1,0:T(8,128)(2,1)S(1)} %get-tuple-element.15), channel_id=1, source_target_pairs={{0,10},{1,11},{2,0},{3,1},{4,2},{5,3},{6,4},{7,5},{8,6},{9,7},{10,... | collective-permute-start | bytes 393224 | tf_op jit(solution)/shard_map/ppermute | solution.py:128
  113.9 3.4 %products.3.refs_4_ = bf16[12,128,128]{2,1,0:T(8,128)(2,1)S(1)} custom-call(s32[75,128]{1,0:T(8,128)S(1)} %fusion.1.table, bf16[16,128,128]{2,1,0:T(8,128)(2,1)S(1)} %join.1.own, bf16[16,128,128]{2,1,0:T(8,128)(2,1)S(1)} %collective-permute-done.17.from_low, bf16[16,128,128]{2,1,0:T(8,128)(2,1)S(1)} %collective-permute-done.18.from_high, ...), custom_call_target="tpu_custom_call" | custom-call | flops 805306368 | bytes 4194304 | tf_op jit(solution)/shard_map/products/pallas_call | solution.py:236
  117.3 6.6 %collective-permute-done.20.refs_0_ = bf16[4,128,128]{2,1,0:T(8,128)(2,1)S(1)} collective-permute-done((bf16[4,128,128]{2,1,0:T(8,128)(2,1)S(1)}, bf16[4,128,128]{2,1,0:T(8,128)(2,1)S(1)}, u32[]{:S(2)}, u32[]{:S(2)}) %collective-permute-start.20) | collective-permute-done | bytes 131104 | tf_op jit(solution)/shard_map/ppermute | solution.py:128
  123.9 3.1 %collective-permute-done.21.refs_1_ = bf16[8,128,128]{2,1,0:T(8,128)(2,1)S(1)} collective-permute-done((bf16[8,128,128]{2,1,0:T(8,128)(2,1)S(1)}, bf16[8,128,128]{2,1,0:T(8,128)(2,1)S(1)}, u32[]{:S(2)}, u32[]{:S(2)}) %collective-permute-start.21) | collective-permute-done | bytes 262176 | tf_op jit(solution)/shard_map/ppermute | solution.py:128
  (92 shorter events, 16.2 us)
Async XLA Ops:
  0.0 47.1 %collective-permute-start.9 = (bf16[16,128,128]{2,1,0:T(8,128)(2,1)}, bf16[16,128,128]{2,1,0:T(8,128)(2,1)S(1)}, u32[]{:S(2)}, u32[]{:S(2)}) collective-permute-start(bf16[16,128,128]{2,1,0:T(8,128)(2,1)} %param.5), channel_id=1, source_target_pairs={{0,3},{1,4},{12,15},{13,16},{24,27},{25,28},{36,39},{37,40},{48,51... | collective-permute-start | bytes 1572872 | tf_op jit(solution)/shard_map/ppermute | solution.py:154
  9.3 37.8 %collective-permute-start.10 = (bf16[16,128,128]{2,1,0:T(8,128)(2,1)}, bf16[16,128,128]{2,1,0:T(8,128)(2,1)S(1)}, u32[]{:S(2)}, u32[]{:S(2)}) collective-permute-start(bf16[16,128,128]{2,1,0:T(8,128)(2,1)} %param.5), channel_id=1, source_target_pairs={{0,9},{1,10},{12,21},{13,22},{24,33},{25,34},{36,45},{37,46},{48,5... | collective-permute-start | bytes 1572872 | tf_op jit(solution)/shard_map/ppermute | solution.py:155
  15.6 4.5 %collective-permute-start.2 = (bf16[4,128,128]{2,1,0:T(8,128)(2,1)S(1)}, bf16[4,128,128]{2,1,0:T(8,128)(2,1)S(1)}, u32[]{:S(2)}, u32[]{:S(2)}) collective-permute-start(bf16[4,128,128]{2,1,0:T(8,128)(2,1)S(1)} %get-tuple-element.31), channel_id=1, source_target_pairs={{0,24},{12,36},{1,25},{13,37},{2,26},{14,38},{3,27},{15,39},{4,28}... | collective-permute-start | bytes 393224 | tf_op jit(solution)/shard_map/ppermute | solution.py:138
  16.3 3.8 %collective-permute-start.1 = (bf16[4,128,128]{2,1,0:T(8,128)(2,1)S(1)}, bf16[4,128,128]{2,1,0:T(8,128)(2,1)S(1)}, u32[]{:S(2)}, u32[]{:S(2)}) collective-permute-start(bf16[4,128,128]{2,1,0:T(8,128)(2,1)S(1)} %get-tuple-element.32), channel_id=1, source_target_pairs={{0,48},{12,60},{1,49},{13,61},{2,50},{14,62},{3,51},{15,63},{4,52}... | collective-permute-start | bytes 393224 | tf_op jit(solution)/shard_map/ppermute | solution.py:138
  16.9 3.2 %collective-permute-start = (bf16[4,128,128]{2,1,0:T(8,128)(2,1)S(1)}, bf16[4,128,128]{2,1,0:T(8,128)(2,1)S(1)}, u32[]{:S(2)}, u32[]{:S(2)}) collective-permute-start(bf16[4,128,128]{2,1,0:T(8,128)(2,1)S(1)} %get-tuple-element.33), channel_id=1, source_target_pairs={{0,72},{12,84},{1,73},{13,85},{2,74},{14,86},{3,75},{15,87},{4,76}... | collective-permute-start | bytes 393224 | tf_op jit(solution)/shard_map/ppermute | solution.py:138
  21.1 1.6 %collective-permute-start.4 = (bf16[4,128,128]{2,1,0:T(8,128)(2,1)S(1)}, bf16[4,128,128]{2,1,0:T(8,128)(2,1)S(1)}, u32[]{:S(2)}, u32[]{:S(2)}) collective-permute-start(bf16[4,128,128]{2,1,0:T(8,128)(2,1)S(1)} %select_select_fusion.3), channel_id=1, source_target_pairs={{0,288},{12,300},{24,312},{36,324},{48,336},{60,348},{72,360},{84,... | collective-permute-start | bytes 393224 | tf_op jit(solution)/shard_map/ppermute | solution.py:144
  21.7 0.9 collective-permute-start.3
  22.7 14.5 %collective-permute-start.6 = (bf16[4,128,128]{2,1,0:T(8,128)(2,1)S(1)}, bf16[4,128,128]{2,1,0:T(8,128)(2,1)S(1)}, u32[]{:S(2)}, u32[]{:S(2)}) collective-permute-start(bf16[4,128,128]{2,1,0:T(8,128)(2,1)S(1)} %select_select_fusion.2), channel_id=1, source_target_pairs={{0,96},{12,108},{24,120},{36,132},{48,144},{60,156},{72,168},{84,1... | collective-permute-start | bytes 393224 | tf_op jit(solution)/shard_map/ppermute | solution.py:144
  24.0 13.2 %collective-permute-start.5 = (bf16[4,128,128]{2,1,0:T(8,128)(2,1)S(1)}, bf16[4,128,128]{2,1,0:T(8,128)(2,1)S(1)}, u32[]{:S(2)}, u32[]{:S(2)}) collective-permute-start(bf16[4,128,128]{2,1,0:T(8,128)(2,1)S(1)} %select_select_fusion.2), channel_id=1, source_target_pairs={{0,672},{12,684},{24,696},{36,708},{48,720},{60,732},{72,744},{84,... | collective-permute-start | bytes 393224 | tf_op jit(solution)/shard_map/ppermute | solution.py:144
  37.3 17.5 %collective-permute-start.8 = (bf16[544,128]{1,0:T(8,128)(2,1)S(1)}, bf16[544,128]{1,0:T(8,128)(2,1)S(1)}, u32[]{:S(2)}, u32[]{:S(2)}) collective-permute-start(bf16[544,128]{1,0:T(8,128)(2,1)S(1)} %pad_maximum_fusion.1), channel_id=1, source_target_pairs={{0,4},{1,5},{2,6},{3,7},{4,8},{5,9},{6,10},{7,11},{8,0},{9,1},{10,... | collective-permute-start | bytes 417800 | tf_op jit(solution)/shard_map/ppermute | solution.py:128
  39.2 15.5 %collective-permute-start.7 = (bf16[544,128]{1,0:T(8,128)(2,1)S(1)}, bf16[544,128]{1,0:T(8,128)(2,1)S(1)}, u32[]{:S(2)}, u32[]{:S(2)}) collective-permute-start(bf16[544,128]{1,0:T(8,128)(2,1)S(1)} %pad_maximum_fusion.1), channel_id=1, source_target_pairs={{0,8},{1,9},{2,10},{3,11},{4,0},{5,1},{6,2},{7,3},{8,4},{9,5},{10,... | collective-permute-start | bytes 417800 | tf_op jit(solution)/shard_map/ppermute | solution.py:128
  47.2 15.8 %collective-permute-start.12 = (bf16[8,128,128]{2,1,0:T(8,128)(2,1)S(1)}, bf16[8,128,128]{2,1,0:T(8,128)(2,1)S(1)}, u32[]{:S(2)}, u32[]{:S(2)}) collective-permute-start(bf16[8,128,128]{2,1,0:T(8,128)(2,1)S(1)} %get-tuple-element.29), channel_id=1, source_target_pairs={{9,6},{10,7},{21,18},{22,19},{33,30},{34,31},{45,42},{46,43},{57,5... | collective-permute-start | bytes 786440 | tf_op jit(solution)/shard_map/ppermute | solution.py:163
  47.9 15.1 %collective-permute-start.11 = (bf16[8,128,128]{2,1,0:T(8,128)(2,1)S(1)}, bf16[8,128,128]{2,1,0:T(8,128)(2,1)S(1)}, u32[]{:S(2)}, u32[]{:S(2)}) collective-permute-start(bf16[8,128,128]{2,1,0:T(8,128)(2,1)S(1)} %get-tuple-element.30), channel_id=1, source_target_pairs={{3,6},{4,7},{15,18},{16,19},{27,30},{28,31},{39,42},{40,43},{51,54... | collective-permute-start | bytes 786440 | tf_op jit(solution)/shard_map/ppermute | solution.py:162
  54.9 21.1 %collective-permute-start.15 = (bf16[12,128,128]{2,1,0:T(8,128)(2,1)S(1)}, bf16[12,128,128]{2,1,0:T(8,128)(2,1)S(1)}, u32[]{:S(2)}, u32[]{:S(2)}) collective-permute-start(bf16[12,128,128]{2,1,0:T(8,128)(2,1)S(1)} %pad_maximum_fusion), channel_id=1, source_target_pairs={{0,24},{12,36},{24,48},{36,60},{48,72},{60,84},{72,0},{84,12},{96,... | collective-permute-start | bytes 1179656 | tf_op jit(solution)/shard_map/ppermute | solution.py:132
  58.4 12.6 %collective-permute-start.13 = (bf16[12,128,128]{2,1,0:T(8,128)(2,1)S(1)}, bf16[12,128,128]{2,1,0:T(8,128)(2,1)S(1)}, u32[]{:S(2)}, u32[]{:S(2)}) collective-permute-start(bf16[12,128,128]{2,1,0:T(8,128)(2,1)S(1)} %pad_maximum_fusion), channel_id=1, source_target_pairs={{0,72},{12,84},{24,0},{36,12},{48,24},{60,36},{72,48},{84,60},{96,... | collective-permute-start | bytes 1179656 | tf_op jit(solution)/shard_map/ppermute | solution.py:132
  63.1 21.8 %collective-permute-start.18 = (bf16[16,128,128]{2,1,0:T(8,128)(2,1)S(1)}, bf16[16,128,128]{2,1,0:T(8,128)(2,1)S(1)}, u32[]{:S(2)}, u32[]{:S(2)}) collective-permute-start(bf16[16,128,128]{2,1,0:T(8,128)(2,1)S(1)} %join.1.own), channel_id=1, source_target_pairs={{0,11},{1,0},{3,2},{4,3},{6,5},{7,6},{9,8},{10,9},{12,23},{13,12},... | collective-permute-start | bytes 1572872 | tf_op jit(solution)/shard_map/ppermute | solution.py:177
  67.1 17.8 %collective-permute-start.17 = (bf16[16,128,128]{2,1,0:T(8,128)(2,1)S(1)}, bf16[16,128,128]{2,1,0:T(8,128)(2,1)S(1)}, u32[]{:S(2)}, u32[]{:S(2)}) collective-permute-start(bf16[16,128,128]{2,1,0:T(8,128)(2,1)S(1)} %join.1.own), channel_id=1, source_target_pairs={{0,1},{1,2},{3,4},{4,5},{6,7},{7,8},{9,10},{10,11},{12,13},{13,14}... | collective-permute-start | bytes 1572872 | tf_op jit(solution)/shard_map/ppermute | solution.py:176
  71.0 7.9 %collective-permute-start.14 = (bf16[6,128,128]{2,1,0:T(8,128)(2,1)S(1)}, bf16[6,128,128]{2,1,0:T(8,128)(2,1)S(1)}, u32[]{:S(2)}, u32[]{:S(2)}) collective-permute-start(bf16[6,128,128]{2,1,0:T(8,128)(2,1)S(1)} %slice.131), channel_id=1, source_target_pairs={{0,72},{12,84},{24,0},{36,12},{48,24},{60,36},{72,48},{84,60},{96,... | collective-permute-start | bytes 589832 | tf_op jit(solution)/shard_map/ppermute | solution.py:132
  76.0 8.8 %collective-permute-start.16 = (bf16[6,128,128]{2,1,0:T(8,128)(2,1)S(1)}, bf16[6,128,128]{2,1,0:T(8,128)(2,1)S(1)}, u32[]{:S(2)}, u32[]{:S(2)}) collective-permute-start(bf16[6,128,128]{2,1,0:T(8,128)(2,1)S(1)} %slice.132), channel_id=1, source_target_pairs={{0,24},{12,36},{24,48},{36,60},{48,72},{60,84},{72,0},{84,12},{96,... | collective-permute-start | bytes 589832 | tf_op jit(solution)/shard_map/ppermute | solution.py:132
  84.9 5.3 %collective-permute-start.19 = (bf16[48,128,128]{2,1,0:T(8,128)(2,1)S(1)}, bf16[48,128,128]{2,1,0:T(8,128)(2,1)S(1)}, u32[]{:S(2)}, u32[]{:S(2)}) collective-permute-start(bf16[48,128,128]{2,1,0:T(8,128)(2,1)S(1)} %constant_dynamic-update-slice_fusion.right_own), channel_id=1, source_target_pairs={{0,12},{12,0},{24,36},{36,24},{48,60},{60,48},{72,84},{84,72},{96,... | collective-permute-start | bytes 4718600 | tf_op jit(solution)/shard_map/ppermute | solution.py:181
  97.0 30.1 %collective-permute-start.22 = (bf16[12,128,128]{2,1,0:T(8,128)(2,1)S(1)}, bf16[12,128,128]{2,1,0:T(8,128)(2,1)S(1)}, u32[]{:S(2)}, u32[]{:S(2)}) collective-permute-start(bf16[12,128,128]{2,1,0:T(8,128)(2,1)S(1)} %get-tuple-element.17), channel_id=1, source_target_pairs={{0,11},{1,0},{2,1},{3,2},{4,3},{5,4},{6,5},{7,6},{8,7},{9,8},{10,9... | collective-permute-start | bytes 1179656 | tf_op jit(solution)/shard_map/ppermute | solution.py:128
  102.1 25.0 %collective-permute-start.23 = (bf16[12,128,128]{2,1,0:T(8,128)(2,1)S(1)}, bf16[12,128,128]{2,1,0:T(8,128)(2,1)S(1)}, u32[]{:S(2)}, u32[]{:S(2)}) collective-permute-start(bf16[12,128,128]{2,1,0:T(8,128)(2,1)S(1)} %get-tuple-element.18), channel_id=1, source_target_pairs={{0,1},{1,2},{2,3},{3,4},{4,5},{5,6},{6,7},{7,8},{8,9},{9,10},{10,1... | collective-permute-start | bytes 1179656 | tf_op jit(solution)/shard_map/ppermute | solution.py:128
  104.0 23.0 %collective-permute-start.21 = (bf16[8,128,128]{2,1,0:T(8,128)(2,1)S(1)}, bf16[8,128,128]{2,1,0:T(8,128)(2,1)S(1)}, u32[]{:S(2)}, u32[]{:S(2)}) collective-permute-start(bf16[8,128,128]{2,1,0:T(8,128)(2,1)S(1)} %get-tuple-element.16), channel_id=1, source_target_pairs={{0,2},{1,3},{2,4},{3,5},{4,6},{5,7},{6,8},{7,9},{8,10},{9,11},{10,... | collective-permute-start | bytes 786440 | tf_op jit(solution)/shard_map/ppermute | solution.py:128
  112.0 11.9 %collective-permute-start.20 = (bf16[4,128,128]{2,1,0:T(8,128)(2,1)S(1)}, bf16[4,128,128]{2,1,0:T(8,128)(2,1)S(1)}, u32[]{:S(2)}, u32[]{:S(2)}) collective-permute-start(bf16[4,128,128]{2,1,0:T(8,128)(2,1)S(1)} %get-tuple-element.15), channel_id=1, source_target_pairs={{0,10},{1,11},{2,0},{3,1},{4,2},{5,3},{6,4},{7,5},{8,6},{9,7},{10,... | collective-permute-start | bytes 393224 | tf_op jit(solution)/shard_map/ppermute | solution.py:128
  (4 other events, 96.7 us)

commit v4 on v3

--- a/solution.py
+++ b/solution.py
@@ -171,12 +171,10 @@
         name="join",
     )(jnp.full((1,), third, jnp.int32), own, low, high)
 
-    after, behind = x_shift(held, 1), x_shift(held, 3)
-    half = HELD * QUARTER // 2
+    after, behind, across = x_shift(held, 1), x_shift(held, 3), x_shift(held, 2)
     from_low = lax.ppermute(own, "col", [(z, (z + 1) % 12) for z in range(12) if z % 3 < 2])
     from_high = lax.ppermute(own, "col", [(z, (z - 1) % 12) for z in range(12) if z % 3 < 2])
-    across = [x_shift(after[:half], 1), x_shift(behind[half:], 3)]
-    right_own = jnp.concatenate([held, after] + across + [behind], 0)
+    right_own = jnp.concatenate([held, after, across, behind], 0)
     right_own, from_low, from_high = lax.optimization_barrier((right_own, from_low, from_high))
     right_other = lax.ppermute(right_own, "row", [(i, i ^ 1) for i in range(64)])
     return plans, own, from_low, from_high, right_own, right_other

time: 130 us -> 131 us (level)
  the two profiles are of different devices: /device:TPU:112 before, /device:TPU:80 now
where the time goes in v4:
time: 131 us; the launch traced here: 130 us
  starting transfers between devices  64.8 us (49%)
  waiting for transfers between devices  41.6 us (32%)
  Pallas kernels  15.5 us (12%)
  local copies, waits for them, and re-layouts  3.66 us (3%)
  other arithmetic  3.51 us (3%)
    ppermute x6, starting transfers between devices, shift(): lax.ppermute(value, axis, [(i, (i + hop) % size) for i in range(size)])  23.9 us
    ppermute x6, waiting for transfers between devices, shift(): lax.ppermute(value, axis, [(i, (i + hop) % size) for i in range(size)])  14.9 us
    pallas_call x2, Pallas kernels, products(): pl.pallas_call(functools.partial(product_kernel, hops), out_shape=[jax.Sh...  14.2 us
    ppermute x4, waiting for transfers between devices, spread_chunk(): lax.ppermute(chunk, 'row', [(8 * a + k, 8 * b + k) for a, b in pairs for...  12.6 us
    ppermute x3, starting transfers between devices, x_shift(): lax.ppermute(value, 'row', [(8 * y + 2 * x + q, 8 * y + 2 * ((x - hop) %...  12 us
    ppermute x1, starting transfers between devices, spread(): near = lax.ppermute(a_blocks, 'col', [(0, 3), (1, 4)])  9.26 us
    ppermute x3, waiting for transfers between devices, x_shift(): lax.ppermute(value, 'row', [(8 * y + 2 * x + q, 8 * y + 2 * ((x - hop) %...  5.77 us
    ppermute x1, starting transfers between devices, spread(): far = lax.ppermute(a_blocks, 'col', [(0, 9), (1, 10)])  5.25 us
  transfers between devices with their start and end apart: 23, of which 8 were waited for; matrix products, arithmetic and copies ran while one was open for 6% of the time, Pallas kernels for 4%

profile of v4, /device:TPU:80, one launch (start us, length us, event | category | flops | bytes accessed | tf_op | source)
XLA Modules:
  0.0 129.9 jit_solution(5163230068469854300)
XLA Ops:
  0.0 9.3 %collective-permute-start.9 = (bf16[16,128,128]{2,1,0:T(8,128)(2,1)}, bf16[16,128,128]{2,1,0:T(8,128)(2,1)S(1)}, u32[]{:S(2)}, u32[]{:S(2)}) collective-permute-start(bf16[16,128,128]{2,1,0:T(8,128)(2,1)} %param.5), channel_id=1, source_target_pairs={{0,3},{1,4},{12,15},{13,16},{24,27},{25,28},{36,39},{37,40},{48,51... | collective-permute-start | bytes 1572872 | tf_op jit(solution)/shard_map/ppermute | solution.py:154
  9.3 5.3 %collective-permute-start.10 = (bf16[16,128,128]{2,1,0:T(8,128)(2,1)}, bf16[16,128,128]{2,1,0:T(8,128)(2,1)S(1)}, u32[]{:S(2)}, u32[]{:S(2)}) collective-permute-start(bf16[16,128,128]{2,1,0:T(8,128)(2,1)} %param.5), channel_id=1, source_target_pairs={{0,9},{1,10},{12,21},{13,22},{24,33},{25,34},{36,45},{37,46},{48,5... | collective-permute-start | bytes 1572872 | tf_op jit(solution)/shard_map/ppermute | solution.py:155
  23.4 1.3 collective-permute-start.5
  25.0 12.6 %collective-permute-done.5 = bf16[4,128,128]{2,1,0:T(8,128)(2,1)S(1)} collective-permute-done((bf16[4,128,128]{2,1,0:T(8,128)(2,1)S(1)}, bf16[4,128,128]{2,1,0:T(8,128)(2,1)S(1)}, u32[]{:S(2)}, u32[]{:S(2)}) %collective-permute-start.5) | collective-permute-done | bytes 131104 | tf_op jit(solution)/shard_map/ppermute | solution.py:144
  37.6 1.9 %collective-permute-start.8 = (bf16[544,128]{1,0:T(8,128)(2,1)S(1)}, bf16[544,128]{1,0:T(8,128)(2,1)S(1)}, u32[]{:S(2)}, u32[]{:S(2)}) collective-permute-start(bf16[544,128]{1,0:T(8,128)(2,1)S(1)} %pad_maximum_fusion.1), channel_id=1, source_target_pairs={{0,4},{1,5},{2,6},{3,7},{4,8},{5,9},{6,10},{7,11},{8,0},{9,1},{10,... | collective-permute-start | bytes 417800 | tf_op jit(solution)/shard_map/ppermute | solution.py:128
  39.6 7.8 %collective-permute-start.7 = (bf16[544,128]{1,0:T(8,128)(2,1)S(1)}, bf16[544,128]{1,0:T(8,128)(2,1)S(1)}, u32[]{:S(2)}, u32[]{:S(2)}) collective-permute-start(bf16[544,128]{1,0:T(8,128)(2,1)S(1)} %pad_maximum_fusion.1), channel_id=1, source_target_pairs={{0,8},{1,9},{2,10},{3,11},{4,0},{5,1},{6,2},{7,3},{8,4},{9,5},{10,... | collective-permute-start | bytes 417800 | tf_op jit(solution)/shard_map/ppermute | solution.py:128
  48.9 6.0 %collective-permute-done.8 = bf16[544,128]{1,0:T(8,128)(2,1)S(1)} collective-permute-done((bf16[544,128]{1,0:T(8,128)(2,1)S(1)}, bf16[544,128]{1,0:T(8,128)(2,1)S(1)}, u32[]{:S(2)}, u32[]{:S(2)}) %collective-permute-start.8) | collective-permute-done | bytes 139296 | tf_op jit(solution)/shard_map/ppermute | solution.py:128
  55.1 2.9 %collective-permute-start.15 = (bf16[12,128,128]{2,1,0:T(8,128)(2,1)S(1)}, bf16[12,128,128]{2,1,0:T(8,128)(2,1)S(1)}, u32[]{:S(2)}, u32[]{:S(2)}) collective-permute-start(bf16[12,128,128]{2,1,0:T(8,128)(2,1)S(1)} %pad_maximum_fusion), channel_id=1, source_target_pairs={{0,24},{12,36},{24,48},{36,60},{48,72},{60,84},{72,0},{84,12},{96,... | collective-permute-start | bytes 1179656 | tf_op jit(solution)/shard_map/ppermute | solution.py:132
  58.0 5.2 %collective-permute-start.14 = (bf16[12,128,128]{2,1,0:T(8,128)(2,1)S(1)}, bf16[12,128,128]{2,1,0:T(8,128)(2,1)S(1)}, u32[]{:S(2)}, u32[]{:S(2)}) collective-permute-start(bf16[12,128,128]{2,1,0:T(8,128)(2,1)S(1)} %pad_maximum_fusion), channel_id=1, source_target_pairs={{0,48},{12,60},{24,72},{36,84},{48,0},{60,12},{72,24},{84,36},{96,... | collective-permute-start | bytes 1179656 | tf_op jit(solution)/shard_map/ppermute | solution.py:132
  63.2 3.8 %collective-permute-start.13 = (bf16[12,128,128]{2,1,0:T(8,128)(2,1)S(1)}, bf16[12,128,128]{2,1,0:T(8,128)(2,1)S(1)}, u32[]{:S(2)}, u32[]{:S(2)}) collective-permute-start(bf16[12,128,128]{2,1,0:T(8,128)(2,1)S(1)} %pad_maximum_fusion), channel_id=1, source_target_pairs={{0,72},{12,84},{24,0},{36,12},{48,24},{60,36},{72,48},{84,60},{96,... | collective-permute-start | bytes 1179656 | tf_op jit(solution)/shard_map/ppermute | solution.py:132
  68.2 4.0 %collective-permute-start.17 = (bf16[16,128,128]{2,1,0:T(8,128)(2,1)S(1)}, bf16[16,128,128]{2,1,0:T(8,128)(2,1)S(1)}, u32[]{:S(2)}, u32[]{:S(2)}) collective-permute-start(bf16[16,128,128]{2,1,0:T(8,128)(2,1)S(1)} %join.1.own), channel_id=1, source_target_pairs={{0,11},{1,0},{3,2},{4,3},{6,5},{7,6},{9,8},{10,9},{12,23},{13,12},... | collective-permute-start | bytes 1572872 | tf_op jit(solution)/shard_map/ppermute | solution.py:176
  72.2 1.9 %collective-permute-start.16 = (bf16[16,128,128]{2,1,0:T(8,128)(2,1)S(1)}, bf16[16,128,128]{2,1,0:T(8,128)(2,1)S(1)}, u32[]{:S(2)}, u32[]{:S(2)}) collective-permute-start(bf16[16,128,128]{2,1,0:T(8,128)(2,1)S(1)} %join.1.own), channel_id=1, source_target_pairs={{0,1},{1,2},{3,4},{4,5},{6,7},{7,8},{9,10},{10,11},{12,13},{13,14}... | collective-permute-start | bytes 1572872 | tf_op jit(solution)/shard_map/ppermute | solution.py:175
  74.4 5.8 %collective-permute-done.13 = bf16[12,128,128]{2,1,0:T(8,128)(2,1)S(1)} collective-permute-done((bf16[12,128,128]{2,1,0:T(8,128)(2,1)S(1)}, bf16[12,128,128]{2,1,0:T(8,128)(2,1)S(1)}, u32[]{:S(2)}, u32[]{:S(2)}) %collective-permute-start.13) | collective-permute-done | bytes 393248 | tf_op jit(solution)/shard_map/ppermute | solution.py:132
  80.3 1.5 %collective-permute-done.17.from_high = bf16[16,128,128]{2,1,0:T(8,128)(2,1)S(1)} collective-permute-done((bf16[16,128,128]{2,1,0:T(8,128)(2,1)S(1)}, bf16[16,128,128]{2,1,0:T(8,128)(2,1)S(1)}, u32[]{:S(2)}, u32[]{:S(2)}) %collective-permute-start.17) | collective-permute-done | bytes 524320 | tf_op jit(solution)/shard_map/ppermute | solution.py:176
  81.9 4.1 %collective-permute-done.16.from_low = bf16[16,128,128]{2,1,0:T(8,128)(2,1)S(1)} collective-permute-done((bf16[16,128,128]{2,1,0:T(8,128)(2,1)S(1)}, bf16[16,128,128]{2,1,0:T(8,128)(2,1)S(1)}, u32[]{:S(2)}, u32[]{:S(2)}) %collective-permute-start.16) | collective-permute-done | bytes 524320 | tf_op jit(solution)/shard_map/ppermute | solution.py:175
  86.0 1.9 %collective-permute-start.18 = (bf16[48,128,128]{2,1,0:T(8,128)(2,1)S(1)}, bf16[48,128,128]{2,1,0:T(8,128)(2,1)S(1)}, u32[]{:S(2)}, u32[]{:S(2)}) collective-permute-start(bf16[48,128,128]{2,1,0:T(8,128)(2,1)S(1)} %constant_dynamic-update-slice_fusion.right_own), channel_id=1, source_target_pairs={{0,12},{12,0},{24,36},{36,24},{48,60},{60,48},{72,84},{84,72},{96,... | collective-permute-start | bytes 4718600 | tf_op jit(solution)/shard_map/ppermute | solution.py:179
  88.7 2.6 %collective-permute-done.18.right_other = bf16[48,128,128]{2,1,0:T(8,128)(2,1)S(1)} collective-permute-done((bf16[48,128,128]{2,1,0:T(8,128)(2,1)S(1)}, bf16[48,128,128]{2,1,0:T(8,128)(2,1)S(1)}, u32[]{:S(2)}, u32[]{:S(2)}) %collective-permute-start.18) | collective-permute-done | bytes 1572896 | tf_op jit(solution)/shard_map/ppermute | solution.py:179
  91.3 8.8 %products.2 = (bf16[4,128,128]{2,1,0:T(8,128)(2,1)S(1)}, bf16[8,128,128]{2,1,0:T(8,128)(2,1)S(1)}, bf16[12,128,128]{2,1,0:T(8,128)(2,1)S(1)}, bf16[12,128,128]{2,1,0:T(8,128)(2,1)S(1)}) custom-call(s32[75,128]{1,0:T(8,128)S(1)} %fusion.1.table, bf16[16,128,128]{2,1,0:T(8,128)(2,1)S(1)} %join.1.own, ...), custom_call_target="tpu_custom_call" | custom-call | flops 2415919104 | bytes 4194304 | tf_op jit(solution)/shard_map/products/pallas_call | solution.py:234
  100.1 3.5 %collective-permute-start.21 = (bf16[12,128,128]{2,1,0:T(8,128)(2,1)S(1)}, bf16[12,128,128]{2,1,0:T(8,128)(2,1)S(1)}, u32[]{:S(2)}, u32[]{:S(2)}) collective-permute-start(bf16[12,128,128]{2,1,0:T(8,128)(2,1)S(1)} %get-tuple-element.17), channel_id=1, source_target_pairs={{0,11},{1,0},{2,1},{3,2},{4,3},{5,4},{6,5},{7,6},{8,7},{9,8},{10,9... | collective-permute-start | bytes 1179656 | tf_op jit(solution)/shard_map/ppermute | solution.py:128
  103.6 2.7 %collective-permute-start.22 = (bf16[12,128,128]{2,1,0:T(8,128)(2,1)S(1)}, bf16[12,128,128]{2,1,0:T(8,128)(2,1)S(1)}, u32[]{:S(2)}, u32[]{:S(2)}) collective-permute-start(bf16[12,128,128]{2,1,0:T(8,128)(2,1)S(1)} %get-tuple-element.18), channel_id=1, source_target_pairs={{0,1},{1,2},{2,3},{3,4},{4,5},{5,6},{6,7},{7,8},{8,9},{9,10},{10,1... | collective-permute-start | bytes 1179656 | tf_op jit(solution)/shard_map/ppermute | solution.py:128
  106.3 4.6 %collective-permute-start.20 = (bf16[8,128,128]{2,1,0:T(8,128)(2,1)S(1)}, bf16[8,128,128]{2,1,0:T(8,128)(2,1)S(1)}, u32[]{:S(2)}, u32[]{:S(2)}) collective-permute-start(bf16[8,128,128]{2,1,0:T(8,128)(2,1)S(1)} %get-tuple-element.16), channel_id=1, source_target_pairs={{0,2},{1,3},{2,4},{3,5},{4,6},{5,7},{6,8},{7,9},{8,10},{9,11},{10,... | collective-permute-start | bytes 786440 | tf_op jit(solution)/shard_map/ppermute | solution.py:128
  110.9 3.3 %collective-permute-start.19 = (bf16[4,128,128]{2,1,0:T(8,128)(2,1)S(1)}, bf16[4,128,128]{2,1,0:T(8,128)(2,1)S(1)}, u32[]{:S(2)}, u32[]{:S(2)}) collective-permute-start(bf16[4,128,128]{2,1,0:T(8,128)(2,1)S(1)} %get-tuple-element.15), channel_id=1, source_target_pairs={{0,10},{1,11},{2,0},{3,1},{4,2},{5,3},{6,4},{7,5},{8,6},{9,7},{10,... | collective-permute-start | bytes 393224 | tf_op jit(solution)/shard_map/ppermute | solution.py:128
  114.3 5.4 %products.3.refs_4_ = bf16[12,128,128]{2,1,0:T(8,128)(2,1)S(1)} custom-call(s32[75,128]{1,0:T(8,128)S(1)} %fusion.1.table, bf16[16,128,128]{2,1,0:T(8,128)(2,1)S(1)} %join.1.own, bf16[16,128,128]{2,1,0:T(8,128)(2,1)S(1)} %collective-permute-done.16.from_low, bf16[16,128,128]{2,1,0:T(8,128)(2,1)S(1)} %collective-permute-done.17.from_high, ...), custom_call_target="tpu_custom_call" | custom-call | flops 805306368 | bytes 4194304 | tf_op jit(solution)/shard_map/products/pallas_call | solution.py:234
  120.6 8.0 %collective-permute-done.20.refs_1_ = bf16[8,128,128]{2,1,0:T(8,128)(2,1)S(1)} collective-permute-done((bf16[8,128,128]{2,1,0:T(8,128)(2,1)S(1)}, bf16[8,128,128]{2,1,0:T(8,128)(2,1)S(1)}, u32[]{:S(2)}, u32[]{:S(2)}) %collective-permute-start.20) | collective-permute-done | bytes 262176 | tf_op jit(solution)/shard_map/ppermute | solution.py:128
  (87 shorter events, 14.8 us)
Async XLA Ops:
  0.0 47.4 %copy-start = (bf16[16,128,128]{2,1,0:T(8,128)(2,1)S(1)}, bf16[16,128,128]{2,1,0:T(8,128)(2,1)}, u32[]{:S(2)}) copy-start(bf16[16,128,128]{2,1,0:T(8,128)(2,1)} %param.5) | copy-start | bytes 1572868
  0.0 47.4 %collective-permute-start.9 = (bf16[16,128,128]{2,1,0:T(8,128)(2,1)}, bf16[16,128,128]{2,1,0:T(8,128)(2,1)S(1)}, u32[]{:S(2)}, u32[]{:S(2)}) collective-permute-start(bf16[16,128,128]{2,1,0:T(8,128)(2,1)} %param.5), channel_id=1, source_target_pairs={{0,3},{1,4},{12,15},{13,16},{24,27},{25,28},{36,39},{37,40},{48,51... | collective-permute-start | bytes 1572872 | tf_op jit(solution)/shard_map/ppermute | solution.py:154
  9.3 38.1 %collective-permute-start.10 = (bf16[16,128,128]{2,1,0:T(8,128)(2,1)}, bf16[16,128,128]{2,1,0:T(8,128)(2,1)S(1)}, u32[]{:S(2)}, u32[]{:S(2)}) collective-permute-start(bf16[16,128,128]{2,1,0:T(8,128)(2,1)} %param.5), channel_id=1, source_target_pairs={{0,9},{1,10},{12,21},{13,22},{24,33},{25,34},{36,45},{37,46},{48,5... | collective-permute-start | bytes 1572872 | tf_op jit(solution)/shard_map/ppermute | solution.py:155
  15.6 4.5 %collective-permute-start.2 = (bf16[4,128,128]{2,1,0:T(8,128)(2,1)S(1)}, bf16[4,128,128]{2,1,0:T(8,128)(2,1)S(1)}, u32[]{:S(2)}, u32[]{:S(2)}) collective-permute-start(bf16[4,128,128]{2,1,0:T(8,128)(2,1)S(1)} %get-tuple-element.31), channel_id=1, source_target_pairs={{0,24},{12,36},{1,25},{13,37},{2,26},{14,38},{3,27},{15,39},{4,28}... | collective-permute-start | bytes 393224 | tf_op jit(solution)/shard_map/ppermute | solution.py:138
  16.3 3.8 %collective-permute-start.1 = (bf16[4,128,128]{2,1,0:T(8,128)(2,1)S(1)}, bf16[4,128,128]{2,1,0:T(8,128)(2,1)S(1)}, u32[]{:S(2)}, u32[]{:S(2)}) collective-permute-start(bf16[4,128,128]{2,1,0:T(8,128)(2,1)S(1)} %get-tuple-element.32), channel_id=1, source_target_pairs={{0,48},{12,60},{1,49},{13,61},{2,50},{14,62},{3,51},{15,63},{4,52}... | collective-permute-start | bytes 393224 | tf_op jit(solution)/shard_map/ppermute | solution.py:138
  16.9 3.2 %collective-permute-start = (bf16[4,128,128]{2,1,0:T(8,128)(2,1)S(1)}, bf16[4,128,128]{2,1,0:T(8,128)(2,1)S(1)}, u32[]{:S(2)}, u32[]{:S(2)}) collective-permute-start(bf16[4,128,128]{2,1,0:T(8,128)(2,1)S(1)} %get-tuple-element.33), channel_id=1, source_target_pairs={{0,72},{12,84},{1,73},{13,85},{2,74},{14,86},{3,75},{15,87},{4,76}... | collective-permute-start | bytes 393224 | tf_op jit(solution)/shard_map/ppermute | solution.py:138
  21.1 1.6 %collective-permute-start.4 = (bf16[4,128,128]{2,1,0:T(8,128)(2,1)S(1)}, bf16[4,128,128]{2,1,0:T(8,128)(2,1)S(1)}, u32[]{:S(2)}, u32[]{:S(2)}) collective-permute-start(bf16[4,128,128]{2,1,0:T(8,128)(2,1)S(1)} %select_select_fusion.3), channel_id=1, source_target_pairs={{0,288},{12,300},{24,312},{36,324},{48,336},{60,348},{72,360},{84,... | collective-permute-start | bytes 393224 | tf_op jit(solution)/shard_map/ppermute | solution.py:144
  21.7 0.9 collective-permute-start.3
  22.7 2.3 %collective-permute-start.6 = (bf16[4,128,128]{2,1,0:T(8,128)(2,1)S(1)}, bf16[4,128,128]{2,1,0:T(8,128)(2,1)S(1)}, u32[]{:S(2)}, u32[]{:S(2)}) collective-permute-start(bf16[4,128,128]{2,1,0:T(8,128)(2,1)S(1)} %select_select_fusion.2), channel_id=1, source_target_pairs={{0,96},{12,108},{24,120},{36,132},{48,144},{60,156},{72,168},{84,1... | collective-permute-start | bytes 393224 | tf_op jit(solution)/shard_map/ppermute | solution.py:144
  23.4 14.2 %collective-permute-start.5 = (bf16[4,128,128]{2,1,0:T(8,128)(2,1)S(1)}, bf16[4,128,128]{2,1,0:T(8,128)(2,1)S(1)}, u32[]{:S(2)}, u32[]{:S(2)}) collective-permute-start(bf16[4,128,128]{2,1,0:T(8,128)(2,1)S(1)} %select_select_fusion.2), channel_id=1, source_target_pairs={{0,672},{12,684},{24,696},{36,708},{48,720},{60,732},{72,744},{84,... | collective-permute-start | bytes 393224 | tf_op jit(solution)/shard_map/ppermute | solution.py:144
  37.6 17.3 %collective-permute-start.8 = (bf16[544,128]{1,0:T(8,128)(2,1)S(1)}, bf16[544,128]{1,0:T(8,128)(2,1)S(1)}, u32[]{:S(2)}, u32[]{:S(2)}) collective-permute-start(bf16[544,128]{1,0:T(8,128)(2,1)S(1)} %pad_maximum_fusion.1), channel_id=1, source_target_pairs={{0,4},{1,5},{2,6},{3,7},{4,8},{5,9},{6,10},{7,11},{8,0},{9,1},{10,... | collective-permute-start | bytes 417800 | tf_op jit(solution)/shard_map/ppermute | solution.py:128
  39.6 15.4 %collective-permute-start.7 = (bf16[544,128]{1,0:T(8,128)(2,1)S(1)}, bf16[544,128]{1,0:T(8,128)(2,1)S(1)}, u32[]{:S(2)}, u32[]{:S(2)}) collective-permute-start(bf16[544,128]{1,0:T(8,128)(2,1)S(1)} %pad_maximum_fusion.1), channel_id=1, source_target_pairs={{0,8},{1,9},{2,10},{3,11},{4,0},{5,1},{6,2},{7,3},{8,4},{9,5},{10,... | collective-permute-start | bytes 417800 | tf_op jit(solution)/shard_map/ppermute | solution.py:128
  47.5 20.6 %collective-permute-start.12 = (bf16[8,128,128]{2,1,0:T(8,128)(2,1)S(1)}, bf16[8,128,128]{2,1,0:T(8,128)(2,1)S(1)}, u32[]{:S(2)}, u32[]{:S(2)}) collective-permute-start(bf16[8,128,128]{2,1,0:T(8,128)(2,1)S(1)} %get-tuple-element.29), channel_id=1, source_target_pairs={{9,6},{10,7},{21,18},{22,19},{33,30},{34,31},{45,42},{46,43},{57,5... | collective-permute-start | bytes 786440 | tf_op jit(solution)/shard_map/ppermute | solution.py:163
  48.2 19.9 %collective-permute-start.11 = (bf16[8,128,128]{2,1,0:T(8,128)(2,1)S(1)}, bf16[8,128,128]{2,1,0:T(8,128)(2,1)S(1)}, u32[]{:S(2)}, u32[]{:S(2)}) collective-permute-start(bf16[8,128,128]{2,1,0:T(8,128)(2,1)S(1)} %get-tuple-element.30), channel_id=1, source_target_pairs={{3,6},{4,7},{15,18},{16,19},{27,30},{28,31},{39,42},{40,43},{51,54... | collective-permute-start | bytes 786440 | tf_op jit(solution)/shard_map/ppermute | solution.py:162
  55.1 25.2 %collective-permute-start.15 = (bf16[12,128,128]{2,1,0:T(8,128)(2,1)S(1)}, bf16[12,128,128]{2,1,0:T(8,128)(2,1)S(1)}, u32[]{:S(2)}, u32[]{:S(2)}) collective-permute-start(bf16[12,128,128]{2,1,0:T(8,128)(2,1)S(1)} %pad_maximum_fusion), channel_id=1, source_target_pairs={{0,24},{12,36},{24,48},{36,60},{48,72},{60,84},{72,0},{84,12},{96,... | collective-permute-start | bytes 1179656 | tf_op jit(solution)/shard_map/ppermute | solution.py:132
  58.0 22.2 %collective-permute-start.14 = (bf16[12,128,128]{2,1,0:T(8,128)(2,1)S(1)}, bf16[12,128,128]{2,1,0:T(8,128)(2,1)S(1)}, u32[]{:S(2)}, u32[]{:S(2)}) collective-permute-start(bf16[12,128,128]{2,1,0:T(8,128)(2,1)S(1)} %pad_maximum_fusion), channel_id=1, source_target_pairs={{0,48},{12,60},{24,72},{36,84},{48,0},{60,12},{72,24},{84,36},{96,... | collective-permute-start | bytes 1179656 | tf_op jit(solution)/shard_map/ppermute | solution.py:132
  63.2 16.9 %collective-permute-start.13 = (bf16[12,128,128]{2,1,0:T(8,128)(2,1)S(1)}, bf16[12,128,128]{2,1,0:T(8,128)(2,1)S(1)}, u32[]{:S(2)}, u32[]{:S(2)}) collective-permute-start(bf16[12,128,128]{2,1,0:T(8,128)(2,1)S(1)} %pad_maximum_fusion), channel_id=1, source_target_pairs={{0,72},{12,84},{24,0},{36,12},{48,24},{60,36},{72,48},{84,60},{96,... | collective-permute-start | bytes 1179656 | tf_op jit(solution)/shard_map/ppermute | solution.py:132
  68.2 13.6 %collective-permute-start.17 = (bf16[16,128,128]{2,1,0:T(8,128)(2,1)S(1)}, bf16[16,128,128]{2,1,0:T(8,128)(2,1)S(1)}, u32[]{:S(2)}, u32[]{:S(2)}) collective-permute-start(bf16[16,128,128]{2,1,0:T(8,128)(2,1)S(1)} %join.1.own), channel_id=1, source_target_pairs={{0,11},{1,0},{3,2},{4,3},{6,5},{7,6},{9,8},{10,9},{12,23},{13,12},... | collective-permute-start | bytes 1572872 | tf_op jit(solution)/shard_map/ppermute | solution.py:176
  72.2 13.8 %collective-permute-start.16 = (bf16[16,128,128]{2,1,0:T(8,128)(2,1)S(1)}, bf16[16,128,128]{2,1,0:T(8,128)(2,1)S(1)}, u32[]{:S(2)}, u32[]{:S(2)}) collective-permute-start(bf16[16,128,128]{2,1,0:T(8,128)(2,1)S(1)} %join.1.own), channel_id=1, source_target_pairs={{0,1},{1,2},{3,4},{4,5},{6,7},{7,8},{9,10},{10,11},{12,13},{13,14}... | collective-permute-start | bytes 1572872 | tf_op jit(solution)/shard_map/ppermute | solution.py:175
  86.0 5.3 %collective-permute-start.18 = (bf16[48,128,128]{2,1,0:T(8,128)(2,1)S(1)}, bf16[48,128,128]{2,1,0:T(8,128)(2,1)S(1)}, u32[]{:S(2)}, u32[]{:S(2)}) collective-permute-start(bf16[48,128,128]{2,1,0:T(8,128)(2,1)S(1)} %constant_dynamic-update-slice_fusion.right_own), channel_id=1, source_target_pairs={{0,12},{12,0},{24,36},{36,24},{48,60},{60,48},{72,84},{84,72},{96,... | collective-permute-start | bytes 4718600 | tf_op jit(solution)/shard_map/ppermute | solution.py:179
  100.1 28.5 %collective-permute-start.21 = (bf16[12,128,128]{2,1,0:T(8,128)(2,1)S(1)}, bf16[12,128,128]{2,1,0:T(8,128)(2,1)S(1)}, u32[]{:S(2)}, u32[]{:S(2)}) collective-permute-start(bf16[12,128,128]{2,1,0:T(8,128)(2,1)S(1)} %get-tuple-element.17), channel_id=1, source_target_pairs={{0,11},{1,0},{2,1},{3,2},{4,3},{5,4},{6,5},{7,6},{8,7},{9,8},{10,9... | collective-permute-start | bytes 1179656 | tf_op jit(solution)/shard_map/ppermute | solution.py:128
  103.6 25.0 %collective-permute-start.22 = (bf16[12,128,128]{2,1,0:T(8,128)(2,1)S(1)}, bf16[12,128,128]{2,1,0:T(8,128)(2,1)S(1)}, u32[]{:S(2)}, u32[]{:S(2)}) collective-permute-start(bf16[12,128,128]{2,1,0:T(8,128)(2,1)S(1)} %get-tuple-element.18), channel_id=1, source_target_pairs={{0,1},{1,2},{2,3},{3,4},{4,5},{5,6},{6,7},{7,8},{8,9},{9,10},{10,1... | collective-permute-start | bytes 1179656 | tf_op jit(solution)/shard_map/ppermute | solution.py:128
  106.3 22.3 %collective-permute-start.20 = (bf16[8,128,128]{2,1,0:T(8,128)(2,1)S(1)}, bf16[8,128,128]{2,1,0:T(8,128)(2,1)S(1)}, u32[]{:S(2)}, u32[]{:S(2)}) collective-permute-start(bf16[8,128,128]{2,1,0:T(8,128)(2,1)S(1)} %get-tuple-element.16), channel_id=1, source_target_pairs={{0,2},{1,3},{2,4},{3,5},{4,6},{5,7},{6,8},{7,9},{8,10},{9,11},{10,... | collective-permute-start | bytes 786440 | tf_op jit(solution)/shard_map/ppermute | solution.py:128
  110.9 9.7 %collective-permute-start.19 = (bf16[4,128,128]{2,1,0:T(8,128)(2,1)S(1)}, bf16[4,128,128]{2,1,0:T(8,128)(2,1)S(1)}, u32[]{:S(2)}, u32[]{:S(2)}) collective-permute-start(bf16[4,128,128]{2,1,0:T(8,128)(2,1)S(1)} %get-tuple-element.15), channel_id=1, source_target_pairs={{0,10},{1,11},{2,0},{3,1},{4,2},{5,3},{6,4},{7,5},{8,6},{9,7},{10,... | collective-permute-start | bytes 393224 | tf_op jit(solution)/shard_map/ppermute | solution.py:128
  (3 other events, 32.1 us)
